TPU v7x, 256 devices: a whole 4x4x8 slice. The times are simulated.
256 devices in a mesh: scale: 4 (over z_lo, core), space: 64 (over x, z_hi, y).
Axes of the slice: x: 4, y: 4, z: 8 (z_hi: 4, z_lo: 2; z = z_hi * 2 + z_lo), core: 2. Of those that a mesh axis runs over, the one named last changes fastest.
Arguments:
- query_rows: bfloat16 [25088, 3584], P('space', 'scale'), may hold values from -8 to 8
- key_rows: bfloat16 [25088, 3584], P('space', 'scale'), may hold values from -8 to 8
- value_rows: bfloat16 [25088, 3584], P('space', 'scale'), may hold values from -24 to 24
- scale_index: int32 [512], replicated, may hold values from 0 to 5, as said below
- norm_gain: float32 [3584], P('scale'), may hold values from 0.1 to 1.9
- cotangent: bfloat16 [25088, 3584], P('space', 'scale'), may hold values from -6 to 6
Outputs:
- normed_out: bfloat16 [25088, 3584], P('space', 'scale')
- grad_query: bfloat16 [25088, 3584], P('space', 'scale')
- grad_key: bfloat16 [25088, 3584], P('space', 'scale')
- grad_value: bfloat16 [25088, 3584], P('space', 'scale')
Inputs may be any that keep to these rules, and one draw needn't show every extreme that they name: `scale_index`: never falls along the coarse tokens; every level from 0 to 5 occurs.
All inputs are finite; a program needn't handle non-finite values.
Results may differ from a plain program's by a relative error of at most 0.033.
Values may be sent and summed in bfloat16 or wider, within the bound.
A program may use at most 128 MiB of HBM per device.

v0:
```python
from functools import partial

import jax
import jax.numpy as jnp
from jax import lax
from jax.sharding import PartitionSpec as P

HEAD_DIM = 128
D = 3584
FT_DEV = 384
WIN = 192
LEVELS = 6


NEGATIVE = -1e30


def with_halo(x, sides, width):
    for axis, dim in sides:
        count, length = (lax.axis_size(axis), x.shape[dim])
        up = [(i, (i + 1) % count) for i in range(count - 1)]
        down = [(j, i) for i, j in up]
        last = lax.slice_in_dim(x, length - width, length, axis=dim)
        first = lax.slice_in_dim(x, 0, width, axis=dim)
        before = lax.ppermute(last, axis, up)
        after = lax.ppermute(first, axis, down)
        x = jnp.concatenate([before, x, after], axis=dim)
    return x


def shifted(block, axis, distance):
    devices = range(lax.axis_size(axis))
    route = [(i - distance, i) for i in devices if i - distance in devices]
    return lax.ppermute(block, axis, route)


def head_major(tensor):
    return jnp.moveaxis(tensor.reshape(tensor.shape[0], -1, HEAD_DIM), 1, 0)


def local_forward(allowed, operands):
    query_head, key_head, value_head = operands
    scores = jnp.einsum(
        "qd,kd->qk", query_head, key_head, preferred_element_type=jnp.float32
    ) * HEAD_DIM ** (-0.5)
    row_peaks = jnp.max(jnp.where(allowed, scores, NEGATIVE), axis=1)
    weights = jnp.where(allowed, jnp.exp(scores - row_peaks[:, None]), 0.0)
    totals = jnp.sum(weights, axis=1)
    summed = jnp.dot(weights.astype(jnp.bfloat16), value_head, preferred_element_type=jnp.float32)
    return (row_peaks, totals, summed)


def local_backward(allowed, operands):
    query_head, key_head, value_head, grad_head, log_head, delta_head = operands
    scaling = HEAD_DIM ** (-0.5)
    scores = (
        jnp.einsum("qd,kd->qk", query_head, key_head, preferred_element_type=jnp.float32) * scaling
    )
    row_probs = jnp.where(allowed, jnp.exp(scores - log_head[:, None]), 0.0)
    grad_values = jnp.einsum(
        "qk,qd->kd", row_probs.astype(jnp.bfloat16), grad_head, preferred_element_type=jnp.float32
    )
    grad_probs = jnp.einsum("qd,kd->qk", grad_head, value_head, preferred_element_type=jnp.float32)
    grad_scores = (row_probs * (grad_probs - delta_head[:, None])).astype(jnp.bfloat16)
    grad_queries = jnp.dot(grad_scores, key_head, preferred_element_type=jnp.float32) * scaling
    grad_keys = (
        jnp.einsum("qk,qd->kd", grad_scores, query_head, preferred_element_type=jnp.float32)
        * scaling
    )
    return (grad_queries, grad_keys, grad_values)


def level_mask(scale_index, query_level):
    return (scale_index[None, :] <= query_level[:, None])[:, None, :]


def coarse_forward(queries, query_level, scale_index, running, arrived, first_row):
    row_peaks, totals, summed = running
    key_piece, value_piece = arrived
    piece_rows = key_piece.shape[0]
    allowed = level_mask(scale_index, query_level)
    key_heads = key_piece.reshape(piece_rows, -1, HEAD_DIM)
    value_heads = value_piece.reshape(piece_rows, -1, HEAD_DIM)
    scores = jnp.einsum(
        "rhd,nhd->rhn", queries, key_heads, preferred_element_type=jnp.float32
    ) * HEAD_DIM ** (-0.5)
    block_peaks = jnp.max(jnp.where(allowed, scores, NEGATIVE), axis=2)
    new_peaks = jnp.maximum(row_peaks, block_peaks)
    weights = jnp.where(allowed, jnp.exp(scores - new_peaks[..., None]), 0.0)
    factor = jnp.exp(row_peaks - new_peaks)
    totals = totals * factor + jnp.sum(weights, axis=2)
    summed = summed * factor[..., None] + jnp.einsum(
        "rhn,nhd->rhd",
        weights.astype(jnp.bfloat16),
        value_heads,
        preferred_element_type=jnp.float32,
    )
    return (new_peaks, totals, summed)


def coarse_backward(
    queries, grad_rows, log_totals, deltas, query_level, scale_index, running, arrived, first_row
):
    key_piece, value_piece = arrived
    piece_rows = key_piece.shape[0]
    scaling = HEAD_DIM ** (-0.5)
    allowed = level_mask(scale_index, query_level)
    key_heads = key_piece.reshape(piece_rows, -1, HEAD_DIM)
    value_heads = value_piece.reshape(piece_rows, -1, HEAD_DIM)
    scores = (
        jnp.einsum("rhd,nhd->rhn", queries, key_heads, preferred_element_type=jnp.float32) * scaling
    )
    row_probs = jnp.where(allowed, jnp.exp(scores - log_totals[..., None]), 0.0)
    piece_values = jnp.einsum(
        "rhn,rhd->nhd",
        row_probs.astype(jnp.bfloat16),
        grad_rows,
        preferred_element_type=jnp.float32,
    )
    grad_probs = jnp.einsum(
        "rhd,nhd->rhn", grad_rows, value_heads, preferred_element_type=jnp.float32
    )
    grad_scores = (row_probs * (grad_probs - deltas[..., None])).astype(jnp.bfloat16)
    grad_queries = (
        jnp.einsum("rhn,nhd->rhd", grad_scores, key_heads, preferred_element_type=jnp.float32)
        * scaling
    )
    piece_keys = (
        jnp.einsum("rhn,rhd->nhd", grad_scores, queries, preferred_element_type=jnp.float32)
        * scaling
    )
    return (grad_queries, piece_keys, piece_values)


def on_device(query_rows, key_rows, value_rows, scale_index, norm_gain, cotangent):
    fine_rows = FT_DEV
    window = WIN
    columns = query_rows.shape[1]
    heads_here = columns // HEAD_DIM
    total_rows = query_rows.shape[0]
    coarse_rows = total_rows - fine_rows
    coarse_total = scale_index.shape[0]
    index_here = lax.axis_index("space")
    spaces = lax.axis_size("space")
    queries = query_rows.reshape(total_rows, heads_here, HEAD_DIM)
    mine_levels = lax.dynamic_slice_in_dim(scale_index, index_here * coarse_rows, coarse_rows)
    query_level = jnp.concatenate([jnp.full((fine_rows,), LEVELS, jnp.int32), mine_levels])
    key_value = jnp.stack([key_rows[:fine_rows], value_rows[:fine_rows]])
    rimmed = with_halo(key_value, (("space", 1),), window)
    rim_span = fine_rows + 2 * window
    offsets = jnp.arange(rim_span) - window
    rows_here = jnp.arange(fine_rows)
    global_key = index_here * fine_rows + offsets
    valid_key = (global_key >= 0) & (global_key < spaces * fine_rows)
    near_mask = (jnp.abs(rows_here[:, None] - offsets[None, :]) <= window) & valid_key[None, :]
    fine_queries = head_major(query_rows[:fine_rows])
    rim_keys = head_major(rimmed[0])
    rim_values = head_major(rimmed[1])
    fine_peaks, fine_totals, fine_summed = lax.map(
        partial(local_forward, near_mask), (fine_queries, rim_keys, rim_values)
    )
    start_peaks = jnp.concatenate(
        [fine_peaks.T, jnp.full((coarse_rows, heads_here), NEGATIVE, jnp.float32)], axis=0
    )
    start_totals = jnp.concatenate(
        [fine_totals.T, jnp.zeros((coarse_rows, heads_here), jnp.float32)], axis=0
    )
    start_summed = jnp.concatenate(
        [
            jnp.moveaxis(fine_summed, 0, 1),
            jnp.zeros((coarse_rows, heads_here, HEAD_DIM), jnp.float32),
        ],
        axis=0,
    )
    forward_fold = partial(coarse_forward, queries, query_level, scale_index)
    mine_keys = key_rows[fine_rows:]
    mine_values = value_rows[fine_rows:]
    row_peaks, totals, summed = forward_fold(
        (start_peaks, start_totals, start_summed),
        (
            lax.all_gather(mine_keys, "space", axis=0, tiled=True),
            lax.all_gather(mine_values, "space", axis=0, tiled=True),
        ),
        jnp.int32(0),
    )
    attended = (summed / totals[..., None]).astype(jnp.bfloat16).reshape(total_rows, columns)
    log_totals = row_peaks + jnp.log(totals)
    attended_f = attended.astype(jnp.float32)
    gained = norm_gain * cotangent.astype(jnp.float32)
    squares, crossed = lax.psum(
        (jnp.sum(attended_f * attended_f, axis=1), jnp.sum(gained * attended_f, axis=1)), "scale"
    )
    inverse = lax.rsqrt(squares / D + 1e-06)[:, None]
    normed_out = (attended_f * inverse * norm_gain).astype(jnp.bfloat16)
    coupling = crossed[:, None] / D
    grad_attended = (inverse * gained - attended_f * inverse**3 * coupling).astype(jnp.bfloat16)
    products = grad_attended.astype(jnp.float32) * attended_f
    deltas = jnp.sum(products.reshape(total_rows, heads_here, HEAD_DIM), axis=2)
    grad_rows = grad_attended.reshape(total_rows, heads_here, HEAD_DIM)
    backward_fold = partial(
        coarse_backward, queries, grad_rows, log_totals, deltas, query_level, scale_index
    )
    start_back = (
        jnp.zeros((total_rows, heads_here, HEAD_DIM), jnp.float32),
        jnp.zeros((coarse_total, heads_here, HEAD_DIM), jnp.float32),
        jnp.zeros((coarse_total, heads_here, HEAD_DIM), jnp.float32),
    )
    grad_queries, grad_keys, grad_values = backward_fold(
        start_back,
        (
            lax.all_gather(mine_keys, "space", axis=0, tiled=True),
            lax.all_gather(mine_values, "space", axis=0, tiled=True),
        ),
        jnp.int32(0),
    )
    coarse_grad_keys, coarse_grad_values = (
        lax.psum_scatter(grad_keys, "space", scatter_dimension=0, tiled=True),
        lax.psum_scatter(grad_values, "space", scatter_dimension=0, tiled=True),
    )
    local_queries, local_keys, local_values = lax.map(
        partial(local_backward, near_mask),
        (
            fine_queries,
            rim_keys,
            rim_values,
            head_major(grad_attended[:fine_rows]),
            log_totals[:fine_rows].T,
            deltas[:fine_rows].T,
        ),
    )
    rim_pair = jnp.stack(
        [
            jnp.moveaxis(local_keys, 0, 1).reshape(rim_span, columns),
            jnp.moveaxis(local_values, 0, 1).reshape(rim_span, columns),
        ]
    )
    from_after = shifted(rim_pair[:, :window].astype(jnp.bfloat16), "space", -1).astype(jnp.float32)
    from_before = shifted(rim_pair[:, rim_span - window :].astype(jnp.bfloat16), "space", 1).astype(
        jnp.float32
    )
    fine_pair = rim_pair[:, window : window + fine_rows]
    fine_pair = fine_pair.at[:, :window].add(from_before)
    fine_pair = fine_pair.at[:, fine_rows - window :].add(from_after)
    coarse_pair = jnp.stack(
        [
            coarse_grad_keys.reshape(coarse_rows, columns),
            coarse_grad_values.reshape(coarse_rows, columns),
        ]
    )
    grad_pair = jnp.concatenate([fine_pair, coarse_pair], axis=1).astype(jnp.bfloat16)
    total_queries = grad_queries.at[:fine_rows].add(jnp.moveaxis(local_queries, 0, 1))
    grad_query = total_queries.reshape(total_rows, columns).astype(jnp.bfloat16)
    return (normed_out, grad_query, grad_pair[0], grad_pair[1])


def solution(mesh):
    in_specs = (
        P("space", "scale"),
        P("space", "scale"),
        P("space", "scale"),
        P(),
        P("scale"),
        P("space", "scale"),
    )
    out_specs = (P("space", "scale"), P("space", "scale"), P("space", "scale"), P("space", "scale"))
    return jax.shard_map(
        on_device, mesh=mesh, in_specs=in_specs, out_specs=out_specs, check_vma=False
    )
```

profile of v0, /device:TPU:32, one launch (start us, length us, event | category | flops | bytes accessed | tf_op | source)
XLA Modules:
  0.0 1296.4 jit_solution(2977676395696234188)
XLA Ops:
  15.8 5.4 collective-permute-start
  21.2 208.2 %all_gather.9 = bf16[512,896]{1,0:T(8,128)(2,1)S(1)} all-gather(bf16[8,896]{1,0:T(8,128)(2,1)S(1)} %slice-done.4), channel_id=1, replica_groups=mesh['scale'=4,'space'=64] {'space'}, dimensions={0}, use_global_device_ids=true | all-gather | bytes 931840 | tf_op jit(solution)/shard_map/all_gather | solution.py:182
  229.4 200.8 %all_gather.8 = bf16[512,896]{1,0:T(8,128)(2,1)} all-gather(bf16[8,896]{1,0:T(8,128)(2,1)S(1)} %slice-done.2), channel_id=1, replica_groups=mesh['scale'=4,'space'=64] {'space'}, dimensions={0}, use_global_device_ids=true | all-gather | bytes 931840 | tf_op jit(solution)/shard_map/all_gather | solution.py:181
  436.8 3.5 fusion.56
  443.9 3.0 pad_maximum_fusion.1
  448.2 2.5 copy.121
  453.4 32.5 %while.33 = (s32[]{:T(128)}, f32[7,384]{1,0:T(8,128)S(1)}, f32[7,384]{1,0:T(8,128)S(1)}, f32[7,384,128]{2,1,0:T(8,128)}, bf16[7,384,128]{2,1,0:T(8,128)(2,1)}, /...) while((s32[]{:T(128)}, f32[7,384]{1,0:T(8,128)S(1)}, ...), condition=%wide.region_3.4_spmd.clone, body=%wide.region_0.3_spmd.clone.sunk | while | flops 157187328 | bytes 4259197 | solution.py:159
  486.0 4.6 fusion.63
  490.6 5.0 fusion.90
  496.0 9.7 all-reduce.4
  507.6 5.8 fusion.80
  513.3 2.9 copy.147
  521.0 4.3 fusion.55
  526.9 2.6 multiply_bitcast_fusion
  530.7 57.1 %while.34 = (s32[]{:T(128)}, f32[7,384,128]{2,1,0:T(8,128)}, f32[7,768,128]{1,2,0:T(8,128)}, f32[7,768,128]{1,2,0:T(8,128)}, bf16[7,384,128]{2,1,0:T(8,128)(2,1)...) while((s32[]{:T(128)}, f32[7,384,128]{2,1,0:T(8,128)}, ...), condition=%wide.region_12.13_spmd.clone, body=%wide.region_11.12_spmd.clone.sunk | while | flops 380878848 | bytes 8865169 | solution.py:220
  587.8 3.1 fusion.61
  596.3 4.9 collective-permute-start.2
  610.1 6.5 collective-permute-done.2
  618.7 3.4 fusion.79
  622.1 10.7 scatter-add.11
  635.0 3.7 slice_add_fusion
  638.7 16.2 %scatter-add.14 = f32[2,384,896]{1,2,0:T(8,128)S(1)} dynamic-update-slice(f32[2,384,896]{1,2,0:T(8,128)S(1)} %copy-done.2, f32[2,192,896]{1,2,0:T(8,128)} %slice_add_fusion, s32[]{:T(128)} %constant.153.clone.1, s32[]{:T(128)} %constant.156.clone.1, s32[]{:T(128)} %constant.153.clone.1) | dynamic-update-slice | bytes 2752516 | tf_op jit(solution)/shard_map/scatter-add | solution.py:243
  656.1 248.3 %reduce-scatter.5.cloned.1.call-done = f32[8,7,128]{2,1,0:T(8,128)} async-done(((f32[512,7,128]{2,1,0:T(8,128)}), f32[8,7,128]{2,1,0:T(8,128)}) %reduce-scatter.5.cloned.1.call-update) | async-done | bytes 28688 | tf_op jit(solution)/shard_map/reduce_scatter | solution.py:218
  905.2 379.2 %reduce-scatter.3.cloned.1.call-done = f32[8,7,128]{2,0,1:T(8,128)} async-done(((f32[512,7,128]{2,0,1:T(8,128)}), f32[8,7,128]{2,0,1:T(8,128)}) %reduce-scatter.3.cloned.1.call-update) | async-done | bytes 28688 | tf_op jit(solution)/shard_map/reduce_scatter | solution.py:217
  (208 shorter events, 147.3 us)
Async XLA Ops:
  7.2 897.3 %reduce-scatter.5.cloned.1.call-start = ((), (), s32[]{:S(2)}) async-start(), calls=%async_computation.3 | async-start | bytes 2129920 | tf_op jit(solution)/shard_map/reduce_scatter | solution.py:218
  11.0 10.2 slice-start.4
  13.2 216.2 %slice-start.2 = ((bf16[392,896]{1,0:T(8,128)(2,1)}), bf16[8,896]{1,0:T(8,128)(2,1)S(1)}, s32[]{:S(2)}) async-start(bf16[392,896]{1,0:T(8,128)(2,1)} %param.17), calls=%async_computation.6 | async-start | bytes 28672 | tf_op jit(solution)/shard_map/slice | solution.py:176
  13.2 427.1 %collective-permute-start.1 = (bf16[2,192,896]{2,1,0:T(8,128)(2,1)}, bf16[2,192,896]{2,1,0:T(8,128)(2,1)}, u32[]{:S(2)}, u32[]{:S(2)}) collective-permute-start(bf16[2,192,896]{2,1,0:T(8,128)(2,1)} %copy.116), channel_id=1, source_target_pairs={{1,0},{2,1},{3,2},{4,3},{5,4},{6,5},{7,6},{8,7},{9,8},{10,9},{11,1... | collective-permute-start | bytes 2064392 | tf_op jit(solution)/shard_map/ppermute | solution.py:26
  15.8 425.9 %collective-permute-start = (bf16[2,192,896]{2,1,0:T(8,128)(2,1)}, bf16[2,192,896]{2,1,0:T(8,128)(2,1)}, u32[]{:S(2)}, u32[]{:S(2)}) collective-permute-start(bf16[2,192,896]{2,1,0:T(8,128)(2,1)} %copy.115), channel_id=1, source_target_pairs={{0,1},{1,2},{2,3},{3,4},{4,5},{5,6},{6,7},{7,8},{8,9},{9,10},{10,1... | collective-permute-start | bytes 2064392 | tf_op jit(solution)/shard_map/ppermute | solution.py:25
  21.2 409.0 %slice-start = ((bf16[392,896]{1,0:T(8,128)(2,1)}), bf16[384,896]{1,0:T(8,128)(2,1)S(1)}, s32[]{:S(2)}) async-start(bf16[392,896]{1,0:T(8,128)(2,1)} %param.16), calls=%async_computation.4 | async-start | bytes 1376256 | tf_op jit(solution)/shard_map/slice | solution.py:156
  433.6 2.9 copy-start.14
  434.9 1.8 copy-start.6
  436.5 3.8 copy-start.5
  486.0 4.6 copy-start.11
  486.0 4.6 copy-start.12
  490.6 5.0 copy-start.8
  490.6 5.0 copy-start.13
  507.6 8.8 copy-start.9
  516.3 768.2 %reduce-scatter.3.cloned.1.call-start = ((), (), s32[]{:S(2)}) async-start(), calls=%async_computation.2 | async-start | bytes 1863680 | tf_op jit(solution)/shard_map/reduce_scatter | solution.py:217
  519.2 1.7 copy-start.10
  525.3 1.6 copy-start.3
  592.5 10.2 copy-start.4
  596.3 8.6 copy-start.7
  596.3 20.3 %collective-permute-start.2 = (bf16[2,192,896]{2,1,0:T(8,128)(2,1)}, bf16[2,192,896]{2,1,0:T(8,128)(2,1)}, u32[]{:S(2)}, u32[]{:S(2)}) collective-permute-start(bf16[2,192,896]{2,1,0:T(8,128)(2,1)} %copy.141), channel_id=1, source_target_pairs={{0,1},{1,2},{2,3},{3,4},{4,5},{5,6},{6,7},{7,8},{8,9},{9,10},{10,1... | collective-permute-start | bytes 2064392 | tf_op jit(solution)/shard_map/ppermute | solution.py:34
  601.1 31.7 %collective-permute-start.3 = (bf16[2,192,896]{2,1,0:T(8,128)(2,1)S(1)}, bf16[2,192,896]{2,1,0:T(8,128)(2,1)}, u32[]{:S(2)}, u32[]{:S(2)}) collective-permute-start(bf16[2,192,896]{2,1,0:T(8,128)(2,1)S(1)} %copy.143), channel_id=1, source_target_pairs={{1,0},{2,1},{3,2},{4,3},{5,4},{6,5},{7,6},{8,7},{9,8},{10,9},{11,1... | collective-permute-start | bytes 2064392 | tf_op jit(solution)/shard_map/ppermute | solution.py:34
  602.7 2.5 copy-start.1
  604.9 1.8 copy-start
  635.0 3.7 copy-start.2
  (2 other events, 2.2 us)
Sparse Core Ops, SparseCore 0:
  516.4 388.0 reduce-scatter.4
  907.1 377.3 reduce-scatter.2
where the time goes:
time: 1300 us
  waiting for transfers between devices  634 us (49%)
  blocking collectives  419 us (32%)
  matrix products  101 us (8%)
  local copies, waits for them, and re-layouts  81.3 us (6%)
  other arithmetic  33.7 us (3%)
  between operations  14.4 us (1%)
  starting transfers between devices  13.3 us (1%)
    reduce_scatter x1, waiting for transfers between devices, on_device(): lax.psum_scatter(grad_keys, 'space', scatter_dimension=0, tiled=True)  379 us
    reduce_scatter x1, waiting for transfers between devices, on_device(): lax.psum_scatter(grad_values, 'space', scatter_dimension=0, tiled=True)  248 us
    all_gather x1, blocking collectives, on_device(): lax.all_gather(mine_values, 'space', axis=0, tiled=True)  208 us
    all_gather x1, blocking collectives, on_device(): lax.all_gather(mine_keys, 'space', axis=0, tiled=True)  201 us
  transfers between devices with their start and end apart: 6, of which 3 were waited for; matrix products, arithmetic and copies ran while one was open for 11% of the time, Pallas kernels for 0%

commit v1 on v0

v1 whole, which is shorter than its diff:
```python
import jax
import jax.numpy as jnp
from jax import lax
from jax.experimental import pallas as pl
from jax.experimental.pallas import tpu as pltpu
from jax.sharding import PartitionSpec as P

HEAD_DIM = 128
HEADS = 7
COLS = HEADS * HEAD_DIM
D = 3584
FINE = 384
WIN = 192
RIM = FINE + 2 * WIN
CO = 8
COARSE = 512
LEVELS = 6
SLOTS = 128
BLOCK = 128
SPAN = 512
NEG = -1e30
SCALING = HEAD_DIM ** (-0.5)
LOG2E = 1.4426950408889634
LN2 = 0.6931471805599453
F32 = jnp.float32
BF16 = jnp.bfloat16
MESH = pl.DeviceIdType.MESH

HALO = 0
AG_Y = 4
AG_Z = 7
AG_X = 10
AG_F = 18
STAT = 22
RS_OPP = 25
RS_X = 27
RS_Z = 31
RS_Y = 34
BACK = 37
COPIES = BACK + 2 * HEADS


def nt(a, b):
    return lax.dot_general(a, b, (((1,), (1,)), ((), ())), preferred_element_type=F32)


def nn(a, b):
    return lax.dot_general(a, b, (((1,), (0,)), ((), ())), preferred_element_type=F32)


def tn(a, b):
    return lax.dot_general(a, b, (((0,), (0,)), ((), ())), preferred_element_type=F32)


def head_cols(h):
    return pl.ds(pl.multiple_of(h * HEAD_DIM, HEAD_DIM), HEAD_DIM)


def diagonal(rows):
    slot = lax.broadcasted_iota(jnp.int32, (rows, COLS), 0) // CO
    column = lax.broadcasted_iota(jnp.int32, (rows, COLS), 1) // HEAD_DIM
    return slot == column


def spread(piece):
    return jnp.where(diagonal(SLOTS), jnp.concatenate([piece] * (SLOTS // CO), axis=0), 0.0)


def collect(wide):
    kept = jnp.where(diagonal(SLOTS), wide, 0.0)
    total = kept[0:CO]
    for g in range(1, HEADS):
        total = total + kept[g * CO : (g + 1) * CO]
    return total


def kernel(
    q, k, v, cot, kv16, qc, cotc, gain, lmask,
    of_n, of_q, of_k, of_v, oc,
    krim, vrim, cbuf, kc, vc, masks, gt, ot, dot, logs, deltas, dqt,
    stat, stat_in, qd, dod, gk, gv, dk, dv, own_k, own_v,
    opp_out, opp_in, x_out, x_in, z_out, z_in, y_out, y_in, back_out, back_in,
    send, recv,
):
    t = lax.axis_index("space")
    s = lax.axis_index("scale")
    x, z, y = t // 16, (t // 4) % 4, t % 4

    def at(xx, zz, yy):
        return {"space": xx * 16 + zz * 4 + yy}

    right = {"space": (t + 1) % 64}
    left = {"space": (t + 63) % 64}
    xr, xl = at((x + 1) % 4, z, y), at((x + 3) % 4, z, y)
    ys = [at(x, z, (y + d) % 4) for d in (1, 2, 3)]
    zs = [at(x, (z + d) % 4, y) for d in (1, 2, 3)]
    ss = [{"scale": (s + d) % 4} for d in (1, 2, 3)]

    def copy(src, dst, number, peer):
        return pltpu.make_async_remote_copy(
            src_ref=src, dst_ref=dst, send_sem=send.at[number], recv_sem=recv.at[number],
            device_id=peer, device_id_type=MESH,
        )

    pending = []

    def start(src, dst, number, peer):
        c = copy(src, dst, number, peer)
        c.start()
        pending.append(c)

    barrier = pltpu.get_barrier_semaphore()
    greeted = [left, right, xl, xr] + ys + zs + ss
    for peer in greeted:
        pl.semaphore_signal(barrier, inc=1, device_id=peer, device_id_type=MESH)
    pl.semaphore_wait(barrier, len(greeted))

    cbuf[t] = kv16[...]
    for d in (1, 2, 3):
        start(cbuf.at[t], cbuf.at[t], AG_Y + d - 1, ys[d - 1])
    halves = (
        (k, krim, slice(WIN, 2 * WIN), slice(0, WIN), right),
        (v, vrim, slice(WIN, 2 * WIN), slice(0, WIN), right),
        (k, krim, slice(0, WIN), slice(WIN + FINE, RIM), left),
        (v, vrim, slice(0, WIN), slice(WIN + FINE, RIM), left),
    )
    for n, (src, dst, a, b, peer) in enumerate(halves):
        start(src.at[a], dst.at[b], HALO + n, peer)

    def line(xx, zz):
        return cbuf.at[pl.ds(xx * 16 + zz * 4, 4)]

    for d in (1, 2, 3):
        got = cbuf.at[x * 16 + z * 4 + (y + 4 - d) % 4]
        copy(got, got, AG_Y + d - 1, ys[d - 1]).wait_recv()
    mine = line(x, z)
    for d in (1, 2, 3):
        start(mine, mine, AG_Z + d - 1, zs[d - 1])
    start(mine, mine, AG_X + 0, xr)
    start(mine, mine, AG_X + 4, xl)

    krim[WIN : WIN + FINE] = k[0:FINE]
    vrim[WIN : WIN + FINE] = v[0:FINE]
    row = lax.broadcasted_iota(jnp.int32, (SPAN, BLOCK), 0)
    column = lax.broadcasted_iota(jnp.int32, (SPAN, BLOCK), 1)
    for b in range(3):
        near = (row >= column) & (row - column <= 2 * WIN)
        place = row + b * BLOCK
        here = ((place >= WIN) | (t > 0)) & ((place < WIN + FINE) | (t < 63))
        masks[b] = jnp.where(near & here, 0.0, NEG)

    def prepare(h, _):
        cols = head_cols(h)
        gained = cot[0:FINE, cols].astype(F32) * gain[:, cols]
        for b in range(3):
            gt[h, :, b * BLOCK : (b + 1) * BLOCK] = gained[b * BLOCK : (b + 1) * BLOCK].T
        return 0

    for d in (1, 3, 2):
        block = line(x, (z + 4 - d) % 4)
        copy(block, block, AG_Z + d - 1, zs[d - 1]).wait_recv()
        start(block, block, AG_X + d, xr)
        start(block, block, AG_X + 4 + d, xl)

    lax.fori_loop(0, HEADS, prepare, 0)
    qd[...] = spread(qc[...]).astype(BF16)

    for d in (0, 1, 3, 2):
        zz = (z + 4 - d) % 4
        from_left, from_right = line((x + 3) % 4, zz), line((x + 1) % 4, zz)
        copy(from_left, from_left, AG_X + d, xr).wait_recv()
        if d in (0, 2):
            start(from_left, from_left, AG_F + d, xr)
        copy(from_right, from_right, AG_X + 4 + d, xl).wait_recv()
        if d in (1, 3):
            start(from_right, from_right, AG_F + d, xl)
    for n, (src, dst, a, b, peer) in enumerate(halves):
        copy(src.at[a], dst.at[b], HALO + n, peer).wait_recv()
    for d in (0, 1, 3, 2):
        far = line((x + 2) % 4, (z + 4 - d) % 4)
        copy(far, far, AG_F + d, xr if d in (0, 2) else xl).wait_recv()

    def forward(h, sums):
        cols = head_cols(h)
        both = cbuf[:, :, cols].astype(F32)
        keys = both[:, 0:CO].reshape(COARSE, HEAD_DIM).astype(BF16)
        values = both[:, CO:].reshape(COARSE, HEAD_DIM).astype(BF16)
        kc[:, cols] = keys
        vc[:, cols] = values
        out = []
        for b in range(3):
            rows = slice(b * BLOCK, (b + 1) * BLOCK)
            rim = slice(b * BLOCK, b * BLOCK + SPAN)
            queries = q[rows, cols]
            near = nt(krim[rim, cols], queries) * (SCALING * LOG2E) + masks[b]
            far = nt(keys, queries) * (SCALING * LOG2E)
            peak = jnp.maximum(
                jnp.max(near, axis=0, keepdims=True), jnp.max(far, axis=0, keepdims=True)
            )
            near, far = jnp.exp2(near - peak), jnp.exp2(far - peak)
            total = jnp.sum(near, axis=0, keepdims=True) + jnp.sum(far, axis=0, keepdims=True)
            summed = tn(vrim[rim, cols], near.astype(BF16)) + tn(values, far.astype(BF16))
            attended = (summed / total).astype(BF16)
            ot[h, :, rows] = attended
            logs[h, :, rows] = peak + jnp.log2(total)
            attended = attended.astype(F32)
            squares, crossed = sums[b]
            out.append((
                squares + jnp.sum(attended * attended, axis=0, keepdims=True),
                crossed + jnp.sum(attended * gt[h, :, rows], axis=0, keepdims=True),
            ))
        return tuple(out)

    nothing = jnp.zeros((1, BLOCK), F32)
    sums = lax.fori_loop(0, HEADS, forward, ((nothing, nothing),) * 3)

    scores = nt(qd[...], kc[...]) * (SCALING * LOG2E) + lmask[...]
    peak = jnp.max(scores, axis=1, keepdims=True)
    weights = jnp.exp2(scores - peak)
    total = jnp.sum(weights, axis=1, keepdims=True)
    wide = nn(weights.astype(BF16), vc[...]) / total
    log_c = peak + jnp.log2(total)
    attended_c = collect(wide).astype(BF16).astype(F32)
    gained_c = cotc[...] * gain[...]
    squares_c = jnp.sum(attended_c * attended_c, axis=1, keepdims=True)
    crossed_c = jnp.sum(attended_c * gained_c, axis=1, keepdims=True)

    stat[...] = jnp.zeros_like(stat)
    for b in range(3):
        stat[0:1, b * BLOCK : (b + 1) * BLOCK] = sums[b][0]
        stat[1:2, b * BLOCK : (b + 1) * BLOCK] = sums[b][1]
    stat[8:16, 0:BLOCK] = jnp.broadcast_to(squares_c, (CO, BLOCK))
    stat[8:16, BLOCK : 2 * BLOCK] = jnp.broadcast_to(crossed_c, (CO, BLOCK))
    for d in (1, 2, 3):
        start(stat, stat_in.at[d - 1], STAT + d - 1, ss[d - 1])
    for d in (1, 2, 3):
        copy(stat, stat_in.at[d - 1], STAT + d - 1, ss[d - 1]).wait_recv()
    whole = stat[...] + stat_in[0] + stat_in[1] + stat_in[2]
    inverse = lax.rsqrt(whole[0:1] / D + 1e-06)
    factor = inverse * inverse * inverse * (whole[1:2] / D)
    inverse_c = lax.rsqrt(whole[8:16, 0:1] / D + 1e-06)
    factor_c = inverse_c * inverse_c * inverse_c * (whole[8:16, BLOCK : BLOCK + 1] / D)

    oc[0] = attended_c * inverse_c * gain[...]
    grad_c = (inverse_c * gained_c - attended_c * factor_c).astype(BF16).astype(F32)
    grad_d = spread(grad_c)
    dod[...] = grad_d.astype(BF16)
    delta_c = jnp.sum(grad_d * spread(attended_c), axis=1, keepdims=True)

    def turn(h, _):
        attended = ot[h].astype(F32)
        grad = (inverse * gt[h] - attended * factor).astype(BF16)
        dot[h] = grad
        deltas[h] = jnp.sum(grad.astype(F32) * attended, axis=0, keepdims=True)
        return 0

    lax.fori_loop(0, HEADS, turn, 0)

    scores = nt(qd[...], kc[...]) * (SCALING * LOG2E) + lmask[...]
    probs = jnp.exp2(scores - log_c)
    grad_probs = nt(dod[...], vc[...])
    grad_scores = (probs * (grad_probs - delta_c)).astype(BF16)
    oc[1] = collect(nn(grad_scores, kc[...])) * SCALING
    gk[...] = tn(grad_scores, qd[...])
    gv[...] = tn(probs.astype(BF16), dod[...])

    def coarse_block(j, first):
        rows = pl.ds(pl.multiple_of(j * BLOCK, BLOCK), BLOCK)

        def body(h, _):
            cols = head_cols(h)
            keys, values = kc[rows, cols], vc[rows, cols]
            queries, grads = q[0:FINE, cols], dot[h]
            probs = jnp.exp2(nt(keys, queries) * (SCALING * LOG2E) - logs[h])
            grad_probs = nn(values, grads)
            grad_scores = (probs * (grad_probs - deltas[h])).astype(BF16)
            gv[rows, cols] = gv[rows, cols] + nt(probs.astype(BF16), grads)
            gk[rows, cols] = (gk[rows, cols] + nn(grad_scores, queries)) * SCALING
            part = tn(keys, grad_scores)
            dqt[h] = part if first else dqt[h] + part
            return 0

        lax.fori_loop(0, HEADS, body, 0)
        return rows

    rows = coarse_block((x + 2) % 4, True)
    opp_out[0] = gk[rows].astype(BF16)
    opp_out[1] = gv[rows].astype(BF16)
    start(opp_out.at[0], opp_in.at[0], RS_OPP, xr)
    start(opp_out.at[1], opp_in.at[1], RS_OPP + 1, xl)
    rows_r = coarse_block((x + 1) % 4, False)
    rows_l = coarse_block((x + 3) % 4, False)
    copy(opp_out.at[0], opp_in.at[0], RS_OPP, xr).wait_recv()
    x_out[0] = (gk[rows_r] + opp_in[0].astype(F32)).astype(BF16)
    x_out[1] = gv[rows_r].astype(BF16)
    start(x_out.at[0], x_in.at[0], RS_X, xr)
    start(x_out.at[1], x_in.at[1], RS_X + 1, xr)
    copy(opp_out.at[1], opp_in.at[1], RS_OPP + 1, xl).wait_recv()
    x_out[2] = gk[rows_l].astype(BF16)
    x_out[3] = (gv[rows_l] + opp_in[1].astype(F32)).astype(BF16)
    start(x_out.at[2], x_in.at[2], RS_X + 2, xl)
    start(x_out.at[3], x_in.at[3], RS_X + 3, xl)

    def fine(h, _):
        cols = head_cols(h)
        dk[...] = jnp.zeros_like(dk)
        dv[...] = jnp.zeros_like(dv)
        for b in range(3):
            rows = slice(b * BLOCK, (b + 1) * BLOCK)
            rim = slice(b * BLOCK, b * BLOCK + SPAN)
            keys, values = krim[rim, cols], vrim[rim, cols]
            queries, grads = q[rows, cols], dot[h, :, rows]
            scores = nt(keys, queries) * (SCALING * LOG2E) + masks[b]
            probs = jnp.exp2(scores - logs[h, :, rows])
            grad_probs = nn(values, grads)
            grad_scores = (probs * (grad_probs - deltas[h, :, rows])).astype(BF16)
            dv[rim] = dv[rim] + nt(probs.astype(BF16), grads)
            dk[rim] = dk[rim] + nn(grad_scores, queries)
            dqt[h, :, rows] = dqt[h, :, rows] + tn(keys, grad_scores)
        back_out[0, h, 0] = (dk[WIN + FINE : RIM] * SCALING).astype(BF16)
        back_out[0, h, 1] = dv[WIN + FINE : RIM].astype(BF16)
        back_out[1, h, 0] = (dk[0:WIN] * SCALING).astype(BF16)
        back_out[1, h, 1] = dv[0:WIN].astype(BF16)
        copy(back_out.at[0, h], back_in.at[0, h], BACK + h, right).start()
        copy(back_out.at[1, h], back_in.at[1, h], BACK + HEADS + h, left).start()
        own_k[h] = dk[WIN : WIN + FINE] * SCALING
        own_v[h] = dv[WIN : WIN + FINE]
        return 0

    lax.fori_loop(0, HEADS, fine, 0)
    own = coarse_block(x, False)

    for n in range(4):
        copy(x_out.at[n], x_in.at[n], RS_X + n, xr if n < 2 else xl).wait_recv()
    gk[own] = gk[own] + x_in[0].astype(F32) + x_in[2].astype(F32)
    gv[own] = gv[own] + x_in[1].astype(F32) + x_in[3].astype(F32)

    def piece(zz, yy, size):
        return pl.ds(pl.multiple_of(x * 128 + zz * 32 + yy * CO, size), size)

    for d in (1, 2, 3):
        there = piece((z + d) % 4, 0, 32)
        z_out[d - 1, 0] = gk[there].astype(BF16)
        z_out[d - 1, 1] = gv[there].astype(BF16)
        start(z_out.at[d - 1], z_in.at[d - 1], RS_Z + d - 1, zs[d - 1])

    def finish(h, _):
        cols = head_cols(h)
        for b in range(3):
            rows = slice(b * BLOCK, (b + 1) * BLOCK)
            of_q[rows, cols] = (dqt[h, :, rows] * SCALING).T.astype(BF16)
            normed = ot[h, :, rows].astype(F32) * inverse[:, rows]
            of_n[rows, cols] = (normed.T * gain[:, cols]).astype(BF16)
        return 0

    lax.fori_loop(0, HEADS, finish, 0)

    for d in (1, 2, 3):
        copy(z_out.at[d - 1], z_in.at[d - 1], RS_Z + d - 1, zs[d - 1]).wait_recv()
    here = piece(z, 0, 32)
    for n, total in enumerate((gk, gv)):
        total[here] = (
            total[here]
            + z_in[0, n].astype(F32) + z_in[1, n].astype(F32) + z_in[2, n].astype(F32)
        )
    for d in (1, 2, 3):
        there = piece(z, (y + d) % 4, CO)
        y_out[d - 1, 0] = gk[there]
        y_out[d - 1, 1] = gv[there]
        start(y_out.at[d - 1], y_in.at[d - 1], RS_Y + d - 1, ys[d - 1])

    def fold(h, _):
        cols = head_cols(h)
        copy(back_out.at[0, h], back_in.at[0, h], BACK + h, right).wait()
        copy(back_out.at[1, h], back_in.at[1, h], BACK + HEADS + h, left).wait()
        for side in range(2):
            rows = slice(side * WIN, (side + 1) * WIN)
            of_k[rows, cols] = (own_k[h, rows] + back_in[side, h, 0].astype(F32)).astype(BF16)
            of_v[rows, cols] = (own_v[h, rows] + back_in[side, h, 1].astype(F32)).astype(BF16)
        return 0

    lax.fori_loop(0, HEADS, fold, 0)

    for d in (1, 2, 3):
        copy(y_out.at[d - 1], y_in.at[d - 1], RS_Y + d - 1, ys[d - 1]).wait_recv()
    here = piece(z, y, CO)
    oc[2] = gk[here] + y_in[0, 0] + y_in[1, 0] + y_in[2, 0]
    oc[3] = gv[here] + y_in[0, 1] + y_in[1, 1] + y_in[2, 1]
    for c in pending:
        c.wait_send()


def on_device(query_rows, key_rows, value_rows, scale_index, norm_gain, cotangent):
    index_here = lax.axis_index("space")
    mine = lax.dynamic_slice_in_dim(scale_index, index_here * CO, CO)
    levels = jnp.concatenate([mine] * (SLOTS // CO))
    lmask = jnp.where(scale_index[None, :] <= levels[:, None], 0.0, NEG).astype(F32)
    kv16 = jnp.concatenate([key_rows[FINE:], value_rows[FINE:]])
    fine = jax.ShapeDtypeStruct((FINE, COLS), BF16)
    whole = pl.BlockSpec(memory_space=pltpu.VMEM)
    scratch = [
        pltpu.VMEM((RIM, COLS), BF16),
        pltpu.VMEM((RIM, COLS), BF16),
        pltpu.VMEM((64, 16, COLS), BF16),
        pltpu.VMEM((COARSE, COLS), BF16),
        pltpu.VMEM((COARSE, COLS), BF16),
        pltpu.VMEM((3, SPAN, BLOCK), F32),
        pltpu.VMEM((HEADS, HEAD_DIM, FINE), F32),
        pltpu.VMEM((HEADS, HEAD_DIM, FINE), BF16),
        pltpu.VMEM((HEADS, HEAD_DIM, FINE), BF16),
        pltpu.VMEM((HEADS, 1, FINE), F32),
        pltpu.VMEM((HEADS, 1, FINE), F32),
        pltpu.VMEM((HEADS, HEAD_DIM, FINE), F32),
        pltpu.VMEM((16, FINE), F32),
        pltpu.VMEM((3, 16, FINE), F32),
        pltpu.VMEM((SLOTS, COLS), BF16),
        pltpu.VMEM((SLOTS, COLS), BF16),
        pltpu.VMEM((COARSE, COLS), F32),
        pltpu.VMEM((COARSE, COLS), F32),
        pltpu.VMEM((RIM, HEAD_DIM), F32),
        pltpu.VMEM((RIM, HEAD_DIM), F32),
        pltpu.VMEM((HEADS, FINE, HEAD_DIM), F32),
        pltpu.VMEM((HEADS, FINE, HEAD_DIM), F32),
        pltpu.VMEM((2, BLOCK, COLS), BF16),
        pltpu.VMEM((2, BLOCK, COLS), BF16),
        pltpu.VMEM((4, BLOCK, COLS), BF16),
        pltpu.VMEM((4, BLOCK, COLS), BF16),
        pltpu.VMEM((3, 2, 32, COLS), BF16),
        pltpu.VMEM((3, 2, 32, COLS), BF16),
        pltpu.VMEM((3, 2, CO, COLS), F32),
        pltpu.VMEM((3, 2, CO, COLS), F32),
        pltpu.VMEM((2, HEADS, 2, WIN, HEAD_DIM), BF16),
        pltpu.VMEM((2, HEADS, 2, WIN, HEAD_DIM), BF16),
        pltpu.SemaphoreType.DMA((COPIES,)),
        pltpu.SemaphoreType.DMA((COPIES,)),
    ]
    outs = pl.pallas_call(
        kernel,
        out_shape=[fine] * 4 + [jax.ShapeDtypeStruct((4, CO, COLS), F32)],
        in_specs=[whole] * 9,
        out_specs=[whole] * 5,
        scratch_shapes=scratch,
        compiler_params=pltpu.CompilerParams(
            collective_id=0, has_side_effects=True, vmem_limit_bytes=56 * 1024 * 1024
        ),
    )(
        query_rows, key_rows, value_rows, cotangent, kv16,
        query_rows[FINE:].astype(F32), cotangent[FINE:].astype(F32), norm_gain[None, :], lmask,
    )
    return tuple(
        jnp.concatenate([outs[n], outs[4][n].astype(BF16)], axis=0) for n in range(4)
    )


def solution(mesh):
    both = P("space", "scale")
    return jax.shard_map(
        on_device, mesh=mesh, in_specs=(both, both, both, P(), P("scale"), both),
        out_specs=(both, both, both, both), check_vma=False,
    )
```

time: 1300 us -> 155 us (0.12)
  the two profiles are of different devices: /device:TPU:32 before, /device:TPU:1 now
where the time goes in v1:
time: 155 us; the launch traced here: 154 us
  Pallas kernels  141 us (91%)
  other arithmetic  9.44 us (6%)
  local copies, waits for them, and re-layouts  3.56 us (2%)
    pallas_call x1, Pallas kernels, on_device(): pl.pallas_call(kernel, out_shape=[fine] * 4 + [jax.ShapeDtypeStruct((4, C...  141 us
    concatenate x2, other arithmetic, on_device(): jnp.concatenate([outs[n], outs[4][n].astype(BF16)], axis=0)  3.8 us

profile of v1, /device:TPU:1, one launch (start us, length us, event | category | flops | bytes accessed | tf_op | source)
XLA Modules:
  0.0 154.2 jit_solution(7129209842913842126)
XLA Ops:
  0.6 0.8 dynamic_slice.3
  1.4 0.1 concatenate.19
  1.5 1.3 broadcast_in_dim.13.gain
  2.8 0.7 slice.28
  3.5 0.7 slice.29
  4.2 0.6 pad_maximum_fusion.4.kv16
  4.8 1.3 slice_convert_fusion.1.qc
  6.1 1.3 slice_convert_fusion.cotc
  7.4 1.5 compare_select_fusion.lmask
  8.9 140.6 %shard_map.93 = (bf16[384,896]{1,0:T(8,128)(2,1)}, bf16[384,896]{1,0:T(8,128)(2,1)}, bf16[384,896]{1,0:T(8,128)(2,1)}, bf16[384,896]{1,0:T(8,128)(2,1)}, f32[4,8,896]{2,1,0:T(8,128)}) custom-call(bf16[392,896]{1,0:T(8,128)(2,1)} %q.1, bf16[392,896]{1,0:T(8,128)(2,1)} %k.1, bf16[392,896]{1,0:T(8,128)(2,1)} %v.1, bf16[392,896]{1,0:T(8,128)(2,1)} %cot.1, ...), custom_call_target="tpu_custom_call" | custom-call | tf_op jit(solution)/shard_map/pallas_call | solution.py:437
  149.5 0.9 convert.6
  150.4 0.0 copy-start
  150.4 0.0 copy-start.1
  150.4 2.6 %pad_maximum_fusion.2 = (bf16[392,896]{1,0:T(8,128)(2,1)}, bf16[392,896]{1,0:T(8,128)(2,1)}) fusion(bf16[8,896]{1,0:T(8,128)(2,1)S(1)} %get-tuple-element.15, bf16[384,896]{1,0:T(8,128)(2,1)} %get-tuple-element.12, bf16[8,896]{1,0:T(8,128)(2,1)S(1)} %get-tuple-element.14, bf16[384,896]{1,0:T(8,128)(2,1)} %get-tuple-element.13), kind=kLoop, calls=%fused_computation.2 | loop fusion | flops 2809856 | bytes 2809856 | tf_op jit(solution)/shard_map/concatenate | solution.py:451
  153.0 0.0 copy-done
  153.0 0.0 copy-done.1
  153.0 1.2 pad_maximum_fusion
  (1 shorter events, 0.0 us)
Async XLA Ops:
  150.4 2.6 %copy-start = (bf16[384,896]{1,0:T(8,128)(2,1)S(1)}, bf16[384,896]{1,0:T(8,128)(2,1)}, u32[]{:S(2)}) copy-start(bf16[384,896]{1,0:T(8,128)(2,1)} %get-tuple-element.9) | copy-start | bytes 2064388
  150.4 2.6 %copy-start.1 = (bf16[384,896]{1,0:T(8,128)(2,1)S(1)}, bf16[384,896]{1,0:T(8,128)(2,1)}, u32[]{:S(2)}) copy-start(bf16[384,896]{1,0:T(8,128)(2,1)} %get-tuple-element.11) | copy-start | bytes 2064388

commit v2 on v1

--- a/solution.py
+++ b/solution.py
@@ -26,18 +26,24 @@
 BF16 = jnp.bfloat16
 MESH = pl.DeviceIdType.MESH
 
-HALO = 0
-AG_Y = 4
-AG_Z = 7
-AG_X = 10
-AG_F = 18
-STAT = 22
-RS_OPP = 25
-RS_X = 27
-RS_Z = 31
-RS_Y = 34
-BACK = 37
-COPIES = BACK + 2 * HEADS
+CHUNKS = 4
+CHUNK = WIN // CHUNKS
+HALO_K = 0
+HALO_V = HALO_K + 2
+HOP = HALO_V + 2 * CHUNKS
+AG_Z = HOP + 2 * CHUNKS
+AG_Y = AG_Z + 3
+AG_X = AG_Y + 3
+AG_F = AG_X + 8
+STAT = AG_F + 4
+RS_OPP = STAT + 3
+RS_X = RS_OPP + 2
+RS_Y = RS_X + 4
+RS_Z = RS_Y + 3
+BACK_K = RS_Z + 3
+BACK_V = BACK_K + 2 * HEADS
+BACK_HOP = BACK_V + 2 * HEADS
+COPIES = BACK_HOP + 2 * HEADS
 
 
 def nt(a, b):
@@ -75,12 +81,12 @@
 
 
 def kernel(
-    q, k, v, cot, kv16, qc, cotc, gain, lmask,
-    of_n, of_q, of_k, of_v, oc,
-    krim, vrim, cbuf, kc, vc, masks, gt, ot, dot, logs, deltas, dqt,
-    stat, stat_in, qd, dod, gk, gv, dk, dv, own_k, own_v,
-    opp_out, opp_in, x_out, x_in, z_out, z_in, y_out, y_in, back_out, back_in,
-    send, recv,
+    q, k, v, cot, gain_ref, levels,
+    of_n, of_q, of_k, of_v,
+    krim, vrim, cbuf, kc, vc, masks, lmask, gt, ot, dot, logs, deltas, dqt,
+    stat, stat_in, coarse_row, qd, dod, gk, gv, dk, dv, own_k, own_v,
+    opp_out, opp_in, x_out, x_in, y_out, y_in, z_out, z_in, back_out, back_in,
+    relay, back_relay, send, recv,
 ):
     t = lax.axis_index("space")
     s = lax.axis_index("scale")
@@ -95,11 +101,22 @@
     ys = [at(x, z, (y + d) % 4) for d in (1, 2, 3)]
     zs = [at(x, (z + d) % 4, y) for d in (1, 2, 3)]
     ss = [{"scale": (s + d) % 4} for d in (1, 2, 3)]
-
-    def copy(src, dst, number, peer):
+    carry = [at((x + 1) % 4, (z + 1) % 4, y), at((x + 3) % 4, (z + 3) % 4, y)]
+
+    edges = (y == 3, y == 0)
+    relaying = (y == 0, y == 3)
+    beside = (right, left)
+    first_hop = (at(x, z, 0), at(x, z, 3))
+    last_hop = (
+        at((x + jnp.where(z == 3, 1, 0)) % 4, (z + 1) % 4, 0),
+        at((x + jnp.where(z == 0, 3, 0)) % 4, (z + 3) % 4, 3),
+    )
+
+    def copy(src, dst, number, peer, out_number=None):
         return pltpu.make_async_remote_copy(
-            src_ref=src, dst_ref=dst, send_sem=send.at[number], recv_sem=recv.at[number],
-            device_id=peer, device_id_type=MESH,
+            src_ref=src, dst_ref=dst,
+            send_sem=send.at[number if out_number is None else out_number],
+            recv_sem=recv.at[number], device_id=peer, device_id_type=MESH,
         )
 
     pending = []
@@ -109,38 +126,84 @@
         c.start()
         pending.append(c)
 
+    def depart(side, number, hop, src, via, dst):
+        @pl.when(edges[side])
+        def _():
+            copy(src, via, hop, first_hop[side]).start()
+
+        @pl.when(jnp.logical_not(edges[side]))
+        def _():
+            copy(src, dst, number, beside[side]).start()
+
+    def pass_on(side, number, hop, via, dst):
+        @pl.when(relaying[side])
+        def _():
+            copy(via, via, hop, first_hop[side]).wait_recv()
+            copy(via, dst, number, last_hop[side], hop).start()
+
+    def departed(side, number, hop, src):
+        @pl.when(edges[side] | relaying[side])
+        def _():
+            copy(src, src, hop, beside[side]).wait_send()
+
+        @pl.when(jnp.logical_not(edges[side]))
+        def _():
+            copy(src, src, number, beside[side]).wait_send()
+
     barrier = pltpu.get_barrier_semaphore()
-    greeted = [left, right, xl, xr] + ys + zs + ss
+    greeted = [left, right, xl, xr] + ys + zs + ss + carry
     for peer in greeted:
         pl.semaphore_signal(barrier, inc=1, device_id=peer, device_id_type=MESH)
+
+    def tail(ref):
+        return ref[...].astype(F32)[FINE:]
+
+    gain = gain_ref[...].reshape(1, COLS)
+    mine = x * 16 + y * 4 + z
+    cbuf[mine] = jnp.concatenate([tail(k), tail(v)], axis=0).astype(BF16)
     pl.semaphore_wait(barrier, len(greeted))
 
-    cbuf[t] = kv16[...]
-    for d in (1, 2, 3):
-        start(cbuf.at[t], cbuf.at[t], AG_Y + d - 1, ys[d - 1])
+    for d in (1, 2, 3):
+        start(cbuf.at[mine], cbuf.at[mine], AG_Z + d - 1, zs[d - 1])
+
+    def chunk(side, c):
+        a = c * CHUNK + (WIN if side == 0 else 0)
+        b = c * CHUNK + (0 if side == 0 else WIN + FINE)
+        return (
+            HALO_V + side * CHUNKS + c, HOP + side * CHUNKS + c,
+            v.at[a : a + CHUNK], relay.at[c], vrim.at[b : b + CHUNK],
+        )
+
+    for c in range(CHUNKS):
+        for side in range(2):
+            depart(side, *chunk(side, c))
     halves = (
         (k, krim, slice(WIN, 2 * WIN), slice(0, WIN), right),
-        (v, vrim, slice(WIN, 2 * WIN), slice(0, WIN), right),
         (k, krim, slice(0, WIN), slice(WIN + FINE, RIM), left),
-        (v, vrim, slice(0, WIN), slice(WIN + FINE, RIM), left),
     )
-    for n, (src, dst, a, b, peer) in enumerate(halves):
-        start(src.at[a], dst.at[b], HALO + n, peer)
-
-    def line(xx, zz):
-        return cbuf.at[pl.ds(xx * 16 + zz * 4, 4)]
-
-    for d in (1, 2, 3):
-        got = cbuf.at[x * 16 + z * 4 + (y + 4 - d) % 4]
-        copy(got, got, AG_Y + d - 1, ys[d - 1]).wait_recv()
-    mine = line(x, z)
-    for d in (1, 2, 3):
-        start(mine, mine, AG_Z + d - 1, zs[d - 1])
-    start(mine, mine, AG_X + 0, xr)
-    start(mine, mine, AG_X + 4, xl)
+
+    def pass_chunk(c):
+        for side in range(2):
+            number, hop, _, via, dst = chunk(side, c)
+            pass_on(side, number, hop, via, dst)
+
+    def line(xx, yy):
+        return cbuf.at[pl.ds(xx * 16 + yy * 4, 4)]
 
     krim[WIN : WIN + FINE] = k[0:FINE]
     vrim[WIN : WIN + FINE] = v[0:FINE]
+    for d in (1, 3, 2):
+        got = cbuf.at[x * 16 + y * 4 + (z + 4 - d) % 4]
+        copy(got, got, AG_Z + d - 1, zs[d - 1]).wait_recv()
+    block = line(x, y)
+    for d in (1, 3, 2):
+        start(block, block, AG_Y + d - 1, ys[d - 1])
+    start(block, block, AG_X + 0, xr)
+    start(block, block, AG_X + 4, xl)
+    for n, (src, dst, a, b, peer) in enumerate(halves):
+        start(src.at[a], dst.at[b], HALO_K + n, peer)
+    pass_chunk(0)
+
     row = lax.broadcasted_iota(jnp.int32, (SPAN, BLOCK), 0)
     column = lax.broadcasted_iota(jnp.int32, (SPAN, BLOCK), 1)
     for b in range(3):
@@ -149,35 +212,53 @@
         here = ((place >= WIN) | (t > 0)) & ((place < WIN + FINE) | (t < 63))
         masks[b] = jnp.where(near & here, 0.0, NEG)
 
+    level = jnp.broadcast_to(levels[...].astype(F32).reshape(1, COARSE), (CO, COARSE))
+    lane = lax.broadcasted_iota(jnp.int32, (CO, COARSE), 1)
+    asked = lane == t * CO + lax.broadcasted_iota(jnp.int32, (CO, COARSE), 0)
+    own_level = jnp.sum(jnp.where(asked, level, 0.0), axis=1, keepdims=True)
+    seen = jnp.sum(jnp.where(level <= own_level, 1.0, 0.0), axis=1, keepdims=True)
+    lane = lax.broadcasted_iota(jnp.int32, (SLOTS, COARSE), 1)
+    order = (lane // 128) * 128 + ((lane // 8) % 4) * 32 + ((lane // 32) % 4) * 8 + lane % 8
+    allowed = order.astype(F32) < jnp.concatenate([seen] * (SLOTS // CO), axis=0)
+    lmask[...] = jnp.where(allowed, 0.0, NEG)
+    pass_chunk(1)
+
     def prepare(h, _):
         cols = head_cols(h)
-        gained = cot[0:FINE, cols].astype(F32) * gain[:, cols]
+        gained = cot[0:FINE, cols].astype(F32) * gain_ref[cols].reshape(1, HEAD_DIM)
         for b in range(3):
             gt[h, :, b * BLOCK : (b + 1) * BLOCK] = gained[b * BLOCK : (b + 1) * BLOCK].T
         return 0
 
+    lax.fori_loop(0, HEADS, prepare, 0)
+    qd[...] = spread(tail(q)).astype(BF16)
+
     for d in (1, 3, 2):
-        block = line(x, (z + 4 - d) % 4)
-        copy(block, block, AG_Z + d - 1, zs[d - 1]).wait_recv()
+        block = line(x, (y + 4 - d) % 4)
+        copy(block, block, AG_Y + d - 1, ys[d - 1]).wait_recv()
         start(block, block, AG_X + d, xr)
         start(block, block, AG_X + 4 + d, xl)
-
-    lax.fori_loop(0, HEADS, prepare, 0)
-    qd[...] = spread(qc[...]).astype(BF16)
+    pass_chunk(2)
 
     for d in (0, 1, 3, 2):
-        zz = (z + 4 - d) % 4
-        from_left, from_right = line((x + 3) % 4, zz), line((x + 1) % 4, zz)
+        yy = (y + 4 - d) % 4
+        from_left, from_right = line((x + 3) % 4, yy), line((x + 1) % 4, yy)
         copy(from_left, from_left, AG_X + d, xr).wait_recv()
         if d in (0, 2):
             start(from_left, from_left, AG_F + d, xr)
         copy(from_right, from_right, AG_X + 4 + d, xl).wait_recv()
         if d in (1, 3):
             start(from_right, from_right, AG_F + d, xl)
+        if d == 1:
+            pass_chunk(3)
     for n, (src, dst, a, b, peer) in enumerate(halves):
-        copy(src.at[a], dst.at[b], HALO + n, peer).wait_recv()
+        copy(src.at[a], dst.at[b], HALO_K + n, peer).wait_recv()
+    for c in range(CHUNKS):
+        for side in range(2):
+            number, _, _, _, dst = chunk(side, c)
+            copy(dst, dst, number, beside[side]).wait_recv()
     for d in (0, 1, 3, 2):
-        far = line((x + 2) % 4, (z + 4 - d) % 4)
+        far = line((x + 2) % 4, (y + 4 - d) % 4)
         copy(far, far, AG_F + d, xr if d in (0, 2) else xl).wait_recv()
 
     def forward(h, sums):
@@ -221,7 +302,7 @@
     wide = nn(weights.astype(BF16), vc[...]) / total
     log_c = peak + jnp.log2(total)
     attended_c = collect(wide).astype(BF16).astype(F32)
-    gained_c = cotc[...] * gain[...]
+    gained_c = tail(cot) * gain
     squares_c = jnp.sum(attended_c * attended_c, axis=1, keepdims=True)
     crossed_c = jnp.sum(attended_c * gained_c, axis=1, keepdims=True)
 
@@ -241,7 +322,7 @@
     inverse_c = lax.rsqrt(whole[8:16, 0:1] / D + 1e-06)
     factor_c = inverse_c * inverse_c * inverse_c * (whole[8:16, BLOCK : BLOCK + 1] / D)
 
-    oc[0] = attended_c * inverse_c * gain[...]
+    normed_c = attended_c * inverse_c * gain
     grad_c = (inverse_c * gained_c - attended_c * factor_c).astype(BF16).astype(F32)
     grad_d = spread(grad_c)
     dod[...] = grad_d.astype(BF16)
@@ -260,7 +341,9 @@
     probs = jnp.exp2(scores - log_c)
     grad_probs = nt(dod[...], vc[...])
     grad_scores = (probs * (grad_probs - delta_c)).astype(BF16)
-    oc[1] = collect(nn(grad_scores, kc[...])) * SCALING
+    query_c = collect(nn(grad_scores, kc[...])) * SCALING
+    coarse_row[0] = normed_c
+    coarse_row[1] = query_c
     gk[...] = tn(grad_scores, qd[...])
     gv[...] = tn(probs.astype(BF16), dod[...])
 
@@ -317,86 +400,118 @@
             dv[rim] = dv[rim] + nt(probs.astype(BF16), grads)
             dk[rim] = dk[rim] + nn(grad_scores, queries)
             dqt[h, :, rows] = dqt[h, :, rows] + tn(keys, grad_scores)
-        back_out[0, h, 0] = (dk[WIN + FINE : RIM] * SCALING).astype(BF16)
-        back_out[0, h, 1] = dv[WIN + FINE : RIM].astype(BF16)
-        back_out[1, h, 0] = (dk[0:WIN] * SCALING).astype(BF16)
-        back_out[1, h, 1] = dv[0:WIN].astype(BF16)
-        copy(back_out.at[0, h], back_in.at[0, h], BACK + h, right).start()
-        copy(back_out.at[1, h], back_in.at[1, h], BACK + HEADS + h, left).start()
+        for side in range(2):
+            part = slice(WIN + FINE, RIM) if side == 0 else slice(0, WIN)
+            back_out[side, h, 0] = (dk[part] * SCALING).astype(BF16)
+            back_out[side, h, 1] = dv[part].astype(BF16)
+            depart(side, *back(side, h))
+            copy(
+                back_out.at[side, h, 0], back_in.at[side, h, 0], BACK_K + side * HEADS + h,
+                beside[side],
+            ).start()
         own_k[h] = dk[WIN : WIN + FINE] * SCALING
         own_v[h] = dv[WIN : WIN + FINE]
         return 0
 
+    def back(side, h):
+        return (
+            BACK_V + side * HEADS + h, BACK_HOP + side * HEADS + h,
+            back_out.at[side, h, 1], back_relay.at[h], back_in.at[side, h, 1],
+        )
+
+    def pass_back(first, last):
+        def body(h, _):
+            for side in range(2):
+                number, hop, _, via, dst = back(side, h)
+                pass_on(side, number, hop, via, dst)
+            return 0
+
+        lax.fori_loop(first, last, body, 0)
+
     lax.fori_loop(0, HEADS, fine, 0)
     own = coarse_block(x, False)
+    pass_back(0, 3)
 
     for n in range(4):
         copy(x_out.at[n], x_in.at[n], RS_X + n, xr if n < 2 else xl).wait_recv()
     gk[own] = gk[own] + x_in[0].astype(F32) + x_in[2].astype(F32)
     gv[own] = gv[own] + x_in[1].astype(F32) + x_in[3].astype(F32)
 
-    def piece(zz, yy, size):
-        return pl.ds(pl.multiple_of(x * 128 + zz * 32 + yy * CO, size), size)
-
-    for d in (1, 2, 3):
-        there = piece((z + d) % 4, 0, 32)
-        z_out[d - 1, 0] = gk[there].astype(BF16)
-        z_out[d - 1, 1] = gv[there].astype(BF16)
-        start(z_out.at[d - 1], z_in.at[d - 1], RS_Z + d - 1, zs[d - 1])
+    def piece(yy, zz, size):
+        return pl.ds(pl.multiple_of(x * 128 + yy * 32 + zz * CO, size), size)
+
+    for d in (1, 2, 3):
+        there = piece((y + d) % 4, 0, 32)
+        y_out[d - 1, 0] = gk[there].astype(BF16)
+        y_out[d - 1, 1] = gv[there].astype(BF16)
+        start(y_out.at[d - 1], y_in.at[d - 1], RS_Y + d - 1, ys[d - 1])
+    pass_back(3, 5)
 
     def finish(h, _):
         cols = head_cols(h)
+        own_gain = gain_ref[cols].reshape(1, HEAD_DIM)
+        queries, normed = [], []
         for b in range(3):
             rows = slice(b * BLOCK, (b + 1) * BLOCK)
-            of_q[rows, cols] = (dqt[h, :, rows] * SCALING).T.astype(BF16)
-            normed = ot[h, :, rows].astype(F32) * inverse[:, rows]
-            of_n[rows, cols] = (normed.T * gain[:, cols]).astype(BF16)
+            queries.append((dqt[h, :, rows] * SCALING).T)
+            normed.append((ot[h, :, rows].astype(F32) * inverse[:, rows]).T * own_gain)
+        of_n[:, cols] = jnp.concatenate(normed + [coarse_row[0, :, cols]], axis=0).astype(BF16)
+        of_q[:, cols] = jnp.concatenate(queries + [coarse_row[1, :, cols]], axis=0).astype(BF16)
         return 0
 
     lax.fori_loop(0, HEADS, finish, 0)
-
-    for d in (1, 2, 3):
-        copy(z_out.at[d - 1], z_in.at[d - 1], RS_Z + d - 1, zs[d - 1]).wait_recv()
-    here = piece(z, 0, 32)
+    pass_back(5, 7)
+
+    for d in (1, 2, 3):
+        copy(y_out.at[d - 1], y_in.at[d - 1], RS_Y + d - 1, ys[d - 1]).wait_recv()
+    here = piece(y, 0, 32)
     for n, total in enumerate((gk, gv)):
         total[here] = (
             total[here]
-            + z_in[0, n].astype(F32) + z_in[1, n].astype(F32) + z_in[2, n].astype(F32)
+            + y_in[0, n].astype(F32) + y_in[1, n].astype(F32) + y_in[2, n].astype(F32)
         )
     for d in (1, 2, 3):
-        there = piece(z, (y + d) % 4, CO)
-        y_out[d - 1, 0] = gk[there]
-        y_out[d - 1, 1] = gv[there]
-        start(y_out.at[d - 1], y_in.at[d - 1], RS_Y + d - 1, ys[d - 1])
+        there = piece(y, (z + d) % 4, CO)
+        z_out[d - 1, 0] = gk[there]
+        z_out[d - 1, 1] = gv[there]
+        start(z_out.at[d - 1], z_in.at[d - 1], RS_Z + d - 1, zs[d - 1])
+    for d in (1, 2, 3):
+        copy(z_out.at[d - 1], z_in.at[d - 1], RS_Z + d - 1, zs[d - 1]).wait_recv()
+    here = piece(y, z, CO)
+    coarse_row[0] = gk[here] + z_in[0, 0] + z_in[1, 0] + z_in[2, 0]
+    coarse_row[1] = gv[here] + z_in[0, 1] + z_in[1, 1] + z_in[2, 1]
 
     def fold(h, _):
         cols = head_cols(h)
-        copy(back_out.at[0, h], back_in.at[0, h], BACK + h, right).wait()
-        copy(back_out.at[1, h], back_in.at[1, h], BACK + HEADS + h, left).wait()
         for side in range(2):
-            rows = slice(side * WIN, (side + 1) * WIN)
-            of_k[rows, cols] = (own_k[h, rows] + back_in[side, h, 0].astype(F32)).astype(BF16)
-            of_v[rows, cols] = (own_v[h, rows] + back_in[side, h, 1].astype(F32)).astype(BF16)
+            number, hop, src, _, dst = back(side, h)
+            copy(dst, dst, number, beside[side]).wait_recv()
+            departed(side, number, hop, src)
+            copy(
+                back_out.at[side, h, 0], back_in.at[side, h, 0], BACK_K + side * HEADS + h,
+                beside[side],
+            ).wait()
+        for n, (mine, target) in enumerate(((own_k, of_k), (own_v, of_v))):
+            parts = [
+                mine[h, side * WIN : (side + 1) * WIN] + back_in[side, h, n].astype(F32)
+                for side in range(2)
+            ]
+            target[:, cols] = jnp.concatenate(
+                parts + [coarse_row[n, :, cols]], axis=0
+            ).astype(BF16)
         return 0
 
     lax.fori_loop(0, HEADS, fold, 0)
-
-    for d in (1, 2, 3):
-        copy(y_out.at[d - 1], y_in.at[d - 1], RS_Y + d - 1, ys[d - 1]).wait_recv()
-    here = piece(z, y, CO)
-    oc[2] = gk[here] + y_in[0, 0] + y_in[1, 0] + y_in[2, 0]
-    oc[3] = gv[here] + y_in[0, 1] + y_in[1, 1] + y_in[2, 1]
+    for c in range(CHUNKS):
+        for side in range(2):
+            number, hop, src, _, _ = chunk(side, c)
+            departed(side, number, hop, src)
     for c in pending:
         c.wait_send()
 
 
 def on_device(query_rows, key_rows, value_rows, scale_index, norm_gain, cotangent):
-    index_here = lax.axis_index("space")
-    mine = lax.dynamic_slice_in_dim(scale_index, index_here * CO, CO)
-    levels = jnp.concatenate([mine] * (SLOTS // CO))
-    lmask = jnp.where(scale_index[None, :] <= levels[:, None], 0.0, NEG).astype(F32)
-    kv16 = jnp.concatenate([key_rows[FINE:], value_rows[FINE:]])
-    fine = jax.ShapeDtypeStruct((FINE, COLS), BF16)
+    full = jax.ShapeDtypeStruct((FINE + CO, COLS), BF16)
     whole = pl.BlockSpec(memory_space=pltpu.VMEM)
     scratch = [
         pltpu.VMEM((RIM, COLS), BF16),
@@ -405,6 +520,7 @@
         pltpu.VMEM((COARSE, COLS), BF16),
         pltpu.VMEM((COARSE, COLS), BF16),
         pltpu.VMEM((3, SPAN, BLOCK), F32),
+        pltpu.VMEM((SLOTS, COARSE), F32),
         pltpu.VMEM((HEADS, HEAD_DIM, FINE), F32),
         pltpu.VMEM((HEADS, HEAD_DIM, FINE), BF16),
         pltpu.VMEM((HEADS, HEAD_DIM, FINE), BF16),
@@ -413,6 +529,7 @@
         pltpu.VMEM((HEADS, HEAD_DIM, FINE), F32),
         pltpu.VMEM((16, FINE), F32),
         pltpu.VMEM((3, 16, FINE), F32),
+        pltpu.VMEM((2, CO, COLS), F32),
         pltpu.VMEM((SLOTS, COLS), BF16),
         pltpu.VMEM((SLOTS, COLS), BF16),
         pltpu.VMEM((COARSE, COLS), F32),
@@ -431,25 +548,21 @@
         pltpu.VMEM((3, 2, CO, COLS), F32),
         pltpu.VMEM((2, HEADS, 2, WIN, HEAD_DIM), BF16),
         pltpu.VMEM((2, HEADS, 2, WIN, HEAD_DIM), BF16),
+        pltpu.VMEM((CHUNKS, CHUNK, COLS), BF16),
+        pltpu.VMEM((HEADS, WIN, HEAD_DIM), BF16),
         pltpu.SemaphoreType.DMA((COPIES,)),
         pltpu.SemaphoreType.DMA((COPIES,)),
     ]
-    outs = pl.pallas_call(
+    return tuple(pl.pallas_call(
         kernel,
-        out_shape=[fine] * 4 + [jax.ShapeDtypeStruct((4, CO, COLS), F32)],
-        in_specs=[whole] * 9,
-        out_specs=[whole] * 5,
+        out_shape=[full] * 4,
+        in_specs=[whole] * 6,
+        out_specs=[whole] * 4,
         scratch_shapes=scratch,
         compiler_params=pltpu.CompilerParams(
             collective_id=0, has_side_effects=True, vmem_limit_bytes=56 * 1024 * 1024
         ),
-    )(
-        query_rows, key_rows, value_rows, cotangent, kv16,
-        query_rows[FINE:].astype(F32), cotangent[FINE:].astype(F32), norm_gain[None, :], lmask,
-    )
-    return tuple(
-        jnp.concatenate([outs[n], outs[4][n].astype(BF16)], axis=0) for n in range(4)
-    )
+    )(query_rows, key_rows, value_rows, cotangent, norm_gain, scale_index))
 
 
 def solution(mesh):

time: 155 us -> 116 us (0.75)
  Pallas kernels: 141 us -> 110 us
  other arithmetic: 9.44 us -> 0 us
  local copies, waits for them, and re-layouts: 3.56 us -> 5.65 us
    pallas_call x1, Pallas kernels: 141 us -> 110 us  [on_device(): pl.pallas_call(kernel, out_shape=[full] * 4, in_specs=[whole] * 6, out_sp...]
    unnamed x4 -> x10, local copies, waits for them, and re-layouts: 0.01 us -> 5.65 us
    concatenate x3 -> x0, other arithmetic: 4.42 us -> none  [the longest x2 3.8 us: on_device(): jnp.concatenate([outs[n], outs[4][n].astype(BF16)], axis=0)]
    convert_element_type x2 -> x0, other arithmetic: 2.65 us -> none  [the longest x1 1.32 us: on_device(): cotangent[FINE:].astype(F32)]
where the time goes in v2:
time: 116 us
  Pallas kernels  110 us (95%)
  local copies, waits for them, and re-layouts  5.65 us (5%)
    pallas_call x1, Pallas kernels, on_device(): pl.pallas_call(kernel, out_shape=[full] * 4, in_specs=[whole] * 6, out_sp...  110 us
    unnamed x10, local copies, waits for them, and re-layouts  5.65 us

profile of v2, /device:TPU:1, one launch (start us, length us, event | category | flops | bytes accessed | tf_op | source)
XLA Modules:
  0.0 116.2 jit_solution(8065206373952070345)
XLA Ops:
  0.6 109.9 %shard_map.93 = (bf16[392,896]{1,0:T(8,128)(2,1)}, bf16[392,896]{1,0:T(8,128)(2,1)}, bf16[392,896]{1,0:T(8,128)(2,1)}, bf16[392,896]{1,0:T(8,128)(2,1)}) custom-call(bf16[392,896]{1,0:T(8,128)(2,1)} %q.1, bf16[392,896]{1,0:T(8,128)(2,1)} %k.1, bf16[392,896]{1,0:T(8,128)(2,1)} %v.1, bf16[392,896]{1,0:T(8,128)(2,1)} %cot.1, f32[896]{0:T(1024)} %gain_ref.1, ...), custom_call_target="tpu_custom_call" | custom-call | tf_op jit(solution)/shard_map/pallas_call | solution.py:556
  110.5 0.0 copy-start.2
  110.5 2.1 %copy.14 = bf16[392,896]{1,0:T(8,128)(2,1)} copy(bf16[392,896]{1,0:T(8,128)(2,1)} %get-tuple-element.8) | data formatting | bytes 1404928
  112.6 0.0 copy-done.2
  112.6 0.0 copy-start.1
  112.6 0.9 copy.15
  113.4 0.5 copy-done.1
  113.9 0.0 copy-start
  113.9 0.9 copy.16
  114.8 0.5 copy-done
  115.3 0.9 copy.17
Async XLA Ops:
  110.5 2.1 %copy-start.2 = (bf16[392,896]{1,0:T(8,128)(2,1)S(1)}, bf16[392,896]{1,0:T(8,128)(2,1)}, u32[]{:S(2)}) copy-start(bf16[392,896]{1,0:T(8,128)(2,1)} %get-tuple-element.9) | copy-start | bytes 2107396
  112.6 1.4 %copy-start.1 = (bf16[392,896]{1,0:T(8,128)(2,1)S(1)}, bf16[392,896]{1,0:T(8,128)(2,1)}, u32[]{:S(2)}) copy-start(bf16[392,896]{1,0:T(8,128)(2,1)} %get-tuple-element.10) | copy-start | bytes 2107396
  113.9 1.4 %copy-start = (bf16[392,896]{1,0:T(8,128)(2,1)S(1)}, bf16[392,896]{1,0:T(8,128)(2,1)}, u32[]{:S(2)}) copy-start(bf16[392,896]{1,0:T(8,128)(2,1)} %get-tuple-element.11) | copy-start | bytes 2107396

commit v3 on v2

--- a/solution.py
+++ b/solution.py
@@ -18,6 +18,8 @@
 SLOTS = 128
 BLOCK = 128
 SPAN = 512
+OWN = ((192, 512), (192, 576), (256, 576))
+HALO = (((0, 192),), ((128, 192), (576, 640)), ((576, 768),))
 NEG = -1e30
 SCALING = HEAD_DIM ** (-0.5)
 LOG2E = 1.4426950408889634
@@ -58,7 +60,15 @@
     return lax.dot_general(a, b, (((0,), (0,)), ((), ())), preferred_element_type=F32)
 
 
+def every_head(body, carry=0, first=0, last=HEADS):
+    for h in range(first, last):
+        carry = body(h, carry)
+    return carry
+
+
 def head_cols(h):
+    if isinstance(h, int):
+        return slice(h * HEAD_DIM, (h + 1) * HEAD_DIM)
     return pl.ds(pl.multiple_of(h * HEAD_DIM, HEAD_DIM), HEAD_DIM)
 
 
@@ -84,7 +94,7 @@
     q, k, v, cot, gain_ref, levels,
     of_n, of_q, of_k, of_v,
     krim, vrim, cbuf, kc, vc, masks, lmask, gt, ot, dot, logs, deltas, dqt,
-    stat, stat_in, coarse_row, qd, dod, gk, gv, dk, dv, own_k, own_v,
+    stat, stat_in, coarse_row, qd, dod, gk, gv, peaks, totals, summed, own_k, own_v,
     opp_out, opp_in, x_out, x_in, y_out, y_in, z_out, z_in, back_out, back_in,
     relay, back_relay, send, recv,
 ):
@@ -192,6 +202,34 @@
 
     krim[WIN : WIN + FINE] = k[0:FINE]
     vrim[WIN : WIN + FINE] = v[0:FINE]
+    row = lax.broadcasted_iota(jnp.int32, (SPAN, BLOCK), 0)
+    column = lax.broadcasted_iota(jnp.int32, (SPAN, BLOCK), 1)
+    for b in range(3):
+        near = (row >= column) & (row - column <= 2 * WIN)
+        place = row + b * BLOCK
+        here = ((place >= WIN) | (t > 0)) & ((place < WIN + FINE) | (t < 63))
+        masks[b] = jnp.where(near & here, 0.0, NEG)
+
+    nothing = jnp.zeros((1, BLOCK), F32)
+
+    def masked(b, first, last):
+        return masks[b, first - b * BLOCK : last - b * BLOCK]
+
+    def own_keys(h, _):
+        cols = head_cols(h)
+        for b in range(3):
+            rows = slice(b * BLOCK, (b + 1) * BLOCK)
+            first, last = OWN[b]
+            scores = nt(krim[first:last, cols], q[rows, cols]) * (SCALING * LOG2E)
+            scores = scores + masked(b, first, last)
+            peak = jnp.max(scores, axis=0, keepdims=True)
+            weights = jnp.exp2(scores - peak)
+            peaks[h, :, rows] = peak
+            totals[h, :, rows] = jnp.sum(weights, axis=0, keepdims=True)
+            summed[h, :, rows] = tn(vrim[first:last, cols], weights.astype(BF16))
+        return 0
+
+    every_head(own_keys, 0, 0, 2)
     for d in (1, 3, 2):
         got = cbuf.at[x * 16 + y * 4 + (z + 4 - d) % 4]
         copy(got, got, AG_Z + d - 1, zs[d - 1]).wait_recv()
@@ -203,14 +241,7 @@
     for n, (src, dst, a, b, peer) in enumerate(halves):
         start(src.at[a], dst.at[b], HALO_K + n, peer)
     pass_chunk(0)
-
-    row = lax.broadcasted_iota(jnp.int32, (SPAN, BLOCK), 0)
-    column = lax.broadcasted_iota(jnp.int32, (SPAN, BLOCK), 1)
-    for b in range(3):
-        near = (row >= column) & (row - column <= 2 * WIN)
-        place = row + b * BLOCK
-        here = ((place >= WIN) | (t > 0)) & ((place < WIN + FINE) | (t < 63))
-        masks[b] = jnp.where(near & here, 0.0, NEG)
+    every_head(own_keys, 0, 2, 4)
 
     level = jnp.broadcast_to(levels[...].astype(F32).reshape(1, COARSE), (CO, COARSE))
     lane = lax.broadcasted_iota(jnp.int32, (CO, COARSE), 1)
@@ -230,15 +261,15 @@
             gt[h, :, b * BLOCK : (b + 1) * BLOCK] = gained[b * BLOCK : (b + 1) * BLOCK].T
         return 0
 
-    lax.fori_loop(0, HEADS, prepare, 0)
-    qd[...] = spread(tail(q)).astype(BF16)
-
     for d in (1, 3, 2):
         block = line(x, (y + 4 - d) % 4)
         copy(block, block, AG_Y + d - 1, ys[d - 1]).wait_recv()
         start(block, block, AG_X + d, xr)
         start(block, block, AG_X + 4 + d, xl)
     pass_chunk(2)
+    every_head(own_keys, 0, 4, HEADS)
+    every_head(prepare, 0, 0, HEADS)
+    qd[...] = spread(tail(q)).astype(BF16)
 
     for d in (0, 1, 3, 2):
         yy = (y + 4 - d) % 4
@@ -251,49 +282,30 @@
             start(from_right, from_right, AG_F + d, xl)
         if d == 1:
             pass_chunk(3)
-    for n, (src, dst, a, b, peer) in enumerate(halves):
-        copy(src.at[a], dst.at[b], HALO_K + n, peer).wait_recv()
-    for c in range(CHUNKS):
-        for side in range(2):
-            number, _, _, _, dst = chunk(side, c)
-            copy(dst, dst, number, beside[side]).wait_recv()
     for d in (0, 1, 3, 2):
         far = line((x + 2) % 4, (y + 4 - d) % 4)
         copy(far, far, AG_F + d, xr if d in (0, 2) else xl).wait_recv()
 
-    def forward(h, sums):
+    def coarse_keys(h, _):
         cols = head_cols(h)
         both = cbuf[:, :, cols].astype(F32)
         keys = both[:, 0:CO].reshape(COARSE, HEAD_DIM).astype(BF16)
         values = both[:, CO:].reshape(COARSE, HEAD_DIM).astype(BF16)
         kc[:, cols] = keys
         vc[:, cols] = values
-        out = []
         for b in range(3):
             rows = slice(b * BLOCK, (b + 1) * BLOCK)
-            rim = slice(b * BLOCK, b * BLOCK + SPAN)
-            queries = q[rows, cols]
-            near = nt(krim[rim, cols], queries) * (SCALING * LOG2E) + masks[b]
-            far = nt(keys, queries) * (SCALING * LOG2E)
-            peak = jnp.maximum(
-                jnp.max(near, axis=0, keepdims=True), jnp.max(far, axis=0, keepdims=True)
-            )
-            near, far = jnp.exp2(near - peak), jnp.exp2(far - peak)
-            total = jnp.sum(near, axis=0, keepdims=True) + jnp.sum(far, axis=0, keepdims=True)
-            summed = tn(vrim[rim, cols], near.astype(BF16)) + tn(values, far.astype(BF16))
-            attended = (summed / total).astype(BF16)
-            ot[h, :, rows] = attended
-            logs[h, :, rows] = peak + jnp.log2(total)
-            attended = attended.astype(F32)
-            squares, crossed = sums[b]
-            out.append((
-                squares + jnp.sum(attended * attended, axis=0, keepdims=True),
-                crossed + jnp.sum(attended * gt[h, :, rows], axis=0, keepdims=True),
-            ))
-        return tuple(out)
-
-    nothing = jnp.zeros((1, BLOCK), F32)
-    sums = lax.fori_loop(0, HEADS, forward, ((nothing, nothing),) * 3)
+            scores = nt(keys, q[rows, cols]) * (SCALING * LOG2E)
+            before = peaks[h, :, rows]
+            peak = jnp.maximum(before, jnp.max(scores, axis=0, keepdims=True))
+            weights = jnp.exp2(scores - peak)
+            scale = jnp.exp2(before - peak)
+            peaks[h, :, rows] = peak
+            totals[h, :, rows] = totals[h, :, rows] * scale + jnp.sum(weights, axis=0, keepdims=True)
+            summed[h, :, rows] = summed[h, :, rows] * scale + tn(values, weights.astype(BF16))
+        return 0
+
+    every_head(coarse_keys, 0, 0, HEADS)
 
     scores = nt(qd[...], kc[...]) * (SCALING * LOG2E) + lmask[...]
     peak = jnp.max(scores, axis=1, keepdims=True)
@@ -305,6 +317,44 @@
     gained_c = tail(cot) * gain
     squares_c = jnp.sum(attended_c * attended_c, axis=1, keepdims=True)
     crossed_c = jnp.sum(attended_c * gained_c, axis=1, keepdims=True)
+
+    for n, (src, dst, a, b, peer) in enumerate(halves):
+        copy(src.at[a], dst.at[b], HALO_K + n, peer).wait_recv()
+    for c in range(CHUNKS):
+        for side in range(2):
+            number, _, _, _, dst = chunk(side, c)
+            copy(dst, dst, number, beside[side]).wait_recv()
+
+    def halo_keys(h, sums):
+        cols = head_cols(h)
+        out = []
+        for b in range(3):
+            rows = slice(b * BLOCK, (b + 1) * BLOCK)
+            peak = before = peaks[h, :, rows]
+            scores = []
+            for first, last in HALO[b]:
+                part = nt(krim[first:last, cols], q[rows, cols]) * (SCALING * LOG2E)
+                part = part + masked(b, first, last)
+                scores.append(part)
+                peak = jnp.maximum(peak, jnp.max(part, axis=0, keepdims=True))
+            scale = jnp.exp2(before - peak)
+            total, total_out = totals[h, :, rows] * scale, summed[h, :, rows] * scale
+            for (first, last), part in zip(HALO[b], scores):
+                weights = jnp.exp2(part - peak)
+                total = total + jnp.sum(weights, axis=0, keepdims=True)
+                total_out = total_out + tn(vrim[first:last, cols], weights.astype(BF16))
+            attended = (total_out / total).astype(BF16)
+            ot[h, :, rows] = attended
+            logs[h, :, rows] = peak + jnp.log2(total)
+            attended = attended.astype(F32)
+            squares, crossed = sums[b]
+            out.append((
+                squares + jnp.sum(attended * attended, axis=0, keepdims=True),
+                crossed + jnp.sum(attended * gt[h, :, rows], axis=0, keepdims=True),
+            ))
+        return tuple(out)
+
+    sums = every_head(halo_keys, ((nothing, nothing),) * 3, 0, HEADS)
 
     stat[...] = jnp.zeros_like(stat)
     for b in range(3):
@@ -335,7 +385,58 @@
         deltas[h] = jnp.sum(grad.astype(F32) * attended, axis=0, keepdims=True)
         return 0
 
-    lax.fori_loop(0, HEADS, turn, 0)
+    every_head(turn, 0, 0, HEADS)
+
+    def back(side, h):
+        return (
+            BACK_V + side * HEADS + h, BACK_HOP + side * HEADS + h,
+            back_out.at[side, h, 1], back_relay.at[h], back_in.at[side, h, 1],
+        )
+
+    def gradients(h, b, first, last):
+        cols = head_cols(h)
+        rows = slice(b * BLOCK, (b + 1) * BLOCK)
+        keys, values = krim[first:last, cols], vrim[first:last, cols]
+        queries, grads = q[rows, cols], dot[h, :, rows]
+        scores = nt(keys, queries) * (SCALING * LOG2E) + masked(b, first, last)
+        probs = jnp.exp2(scores - logs[h, :, rows])
+        grad_probs = nn(values, grads)
+        grad_scores = (probs * (grad_probs - deltas[h, :, rows])).astype(BF16)
+        return (
+            tn(keys, grad_scores), nn(grad_scores, queries) * SCALING, nt(probs.astype(BF16), grads)
+        )
+
+    def halo_grads(h, _):
+        q0, k0, v0 = gradients(h, 0, 0, 192)
+        q1, k1, v1 = gradients(h, 1, 128, 192)
+        q2, k2, v2 = gradients(h, 1, 576, 640)
+        q3, k3, v3 = gradients(h, 2, 576, 768)
+        dqt[h, :, 0:BLOCK] = q0
+        dqt[h, :, BLOCK : 2 * BLOCK] = q1 + q2
+        dqt[h, :, 2 * BLOCK : FINE] = q3
+        for n, (a, b, c, d) in enumerate(((k0, k1, k2, k3), (v0, v1, v2, v3))):
+            back_out[1, h, n, 0:128] = a[0:128].astype(BF16)
+            back_out[1, h, n, 128:192] = (a[128:192] + b).astype(BF16)
+            back_out[0, h, n, 0:64] = (d[0:64] + c).astype(BF16)
+            back_out[0, h, n, 64:192] = d[64:192].astype(BF16)
+        for side in range(2):
+            depart(side, *back(side, h))
+            copy(
+                back_out.at[side, h, 0], back_in.at[side, h, 0], BACK_K + side * HEADS + h,
+                beside[side],
+            ).start()
+        return 0
+
+    def pass_back(first, last):
+        def body(h, _):
+            for side in range(2):
+                number, hop, _, via, dst = back(side, h)
+                pass_on(side, number, hop, via, dst)
+            return 0
+
+        every_head(body, 0, first, last)
+
+    every_head(halo_grads, 0, 0, HEADS)
 
     scores = nt(qd[...], kc[...]) * (SCALING * LOG2E) + lmask[...]
     probs = jnp.exp2(scores - log_c)
@@ -347,7 +448,7 @@
     gk[...] = tn(grad_scores, qd[...])
     gv[...] = tn(probs.astype(BF16), dod[...])
 
-    def coarse_block(j, first):
+    def coarse_block(j):
         rows = pl.ds(pl.multiple_of(j * BLOCK, BLOCK), BLOCK)
 
         def body(h, _):
@@ -360,19 +461,21 @@
             gv[rows, cols] = gv[rows, cols] + nt(probs.astype(BF16), grads)
             gk[rows, cols] = (gk[rows, cols] + nn(grad_scores, queries)) * SCALING
             part = tn(keys, grad_scores)
-            dqt[h] = part if first else dqt[h] + part
+            dqt[h] = dqt[h] + part
             return 0
 
-        lax.fori_loop(0, HEADS, body, 0)
+        every_head(body, 0, 0, HEADS)
         return rows
 
-    rows = coarse_block((x + 2) % 4, True)
+    rows = coarse_block((x + 2) % 4)
     opp_out[0] = gk[rows].astype(BF16)
     opp_out[1] = gv[rows].astype(BF16)
     start(opp_out.at[0], opp_in.at[0], RS_OPP, xr)
     start(opp_out.at[1], opp_in.at[1], RS_OPP + 1, xl)
-    rows_r = coarse_block((x + 1) % 4, False)
-    rows_l = coarse_block((x + 3) % 4, False)
+    pass_back(0, 2)
+    rows_r = coarse_block((x + 1) % 4)
+    pass_back(2, 4)
+    rows_l = coarse_block((x + 3) % 4)
     copy(opp_out.at[0], opp_in.at[0], RS_OPP, xr).wait_recv()
     x_out[0] = (gk[rows_r] + opp_in[0].astype(F32)).astype(BF16)
     x_out[1] = gv[rows_r].astype(BF16)
@@ -383,54 +486,29 @@
     x_out[3] = (gv[rows_l] + opp_in[1].astype(F32)).astype(BF16)
     start(x_out.at[2], x_in.at[2], RS_X + 2, xl)
     start(x_out.at[3], x_in.at[3], RS_X + 3, xl)
-
-    def fine(h, _):
-        cols = head_cols(h)
-        dk[...] = jnp.zeros_like(dk)
-        dv[...] = jnp.zeros_like(dv)
+    pass_back(4, 6)
+
+    own = coarse_block(x)
+    pass_back(6, 7)
+
+    def own_grads(h, _):
         for b in range(3):
+            first, last = OWN[b]
+            part, part_k, part_v = gradients(h, b, first, last)
             rows = slice(b * BLOCK, (b + 1) * BLOCK)
-            rim = slice(b * BLOCK, b * BLOCK + SPAN)
-            keys, values = krim[rim, cols], vrim[rim, cols]
-            queries, grads = q[rows, cols], dot[h, :, rows]
-            scores = nt(keys, queries) * (SCALING * LOG2E) + masks[b]
-            probs = jnp.exp2(scores - logs[h, :, rows])
-            grad_probs = nn(values, grads)
-            grad_scores = (probs * (grad_probs - deltas[h, :, rows])).astype(BF16)
-            dv[rim] = dv[rim] + nt(probs.astype(BF16), grads)
-            dk[rim] = dk[rim] + nn(grad_scores, queries)
-            dqt[h, :, rows] = dqt[h, :, rows] + tn(keys, grad_scores)
-        for side in range(2):
-            part = slice(WIN + FINE, RIM) if side == 0 else slice(0, WIN)
-            back_out[side, h, 0] = (dk[part] * SCALING).astype(BF16)
-            back_out[side, h, 1] = dv[part].astype(BF16)
-            depart(side, *back(side, h))
-            copy(
-                back_out.at[side, h, 0], back_in.at[side, h, 0], BACK_K + side * HEADS + h,
-                beside[side],
-            ).start()
-        own_k[h] = dk[WIN : WIN + FINE] * SCALING
-        own_v[h] = dv[WIN : WIN + FINE]
-        return 0
-
-    def back(side, h):
-        return (
-            BACK_V + side * HEADS + h, BACK_HOP + side * HEADS + h,
-            back_out.at[side, h, 1], back_relay.at[h], back_in.at[side, h, 1],
-        )
-
-    def pass_back(first, last):
-        def body(h, _):
-            for side in range(2):
-                number, hop, _, via, dst = back(side, h)
-                pass_on(side, number, hop, via, dst)
-            return 0
-
-        lax.fori_loop(first, last, body, 0)
-
-    lax.fori_loop(0, HEADS, fine, 0)
-    own = coarse_block(x, False)
-    pass_back(0, 3)
+            dqt[h, :, rows] = dqt[h, :, rows] + part
+            here = slice(first - WIN, last - WIN)
+            if b == 0:
+                own_k[h, here], own_v[h, here] = part_k, part_v
+                rest = slice(last - WIN, FINE)
+                own_k[h, rest] = jnp.zeros((FINE + WIN - last, HEAD_DIM), F32)
+                own_v[h, rest] = jnp.zeros((FINE + WIN - last, HEAD_DIM), F32)
+            else:
+                own_k[h, here] = own_k[h, here] + part_k
+                own_v[h, here] = own_v[h, here] + part_v
+        return 0
+
+    every_head(own_grads, 0, 0, HEADS)
 
     for n in range(4):
         copy(x_out.at[n], x_in.at[n], RS_X + n, xr if n < 2 else xl).wait_recv()
@@ -445,7 +523,6 @@
         y_out[d - 1, 0] = gk[there].astype(BF16)
         y_out[d - 1, 1] = gv[there].astype(BF16)
         start(y_out.at[d - 1], y_in.at[d - 1], RS_Y + d - 1, ys[d - 1])
-    pass_back(3, 5)
 
     def finish(h, _):
         cols = head_cols(h)
@@ -459,8 +536,7 @@
         of_q[:, cols] = jnp.concatenate(queries + [coarse_row[1, :, cols]], axis=0).astype(BF16)
         return 0
 
-    lax.fori_loop(0, HEADS, finish, 0)
-    pass_back(5, 7)
+    every_head(finish, 0, 0, HEADS)
 
     for d in (1, 2, 3):
         copy(y_out.at[d - 1], y_in.at[d - 1], RS_Y + d - 1, ys[d - 1]).wait_recv()
@@ -501,13 +577,26 @@
             ).astype(BF16)
         return 0
 
-    lax.fori_loop(0, HEADS, fold, 0)
+    every_head(fold, 0, 0, HEADS)
     for c in range(CHUNKS):
         for side in range(2):
             number, hop, src, _, _ = chunk(side, c)
             departed(side, number, hop, src)
     for c in pending:
         c.wait_send()
+
+
+def deliver(a, b, c, d, to_a, to_b, to_c, to_d, held, arrive, leave):
+    pairs = ((a, to_a), (b, to_b), (c, to_c), (d, to_d))
+    inward = [pltpu.make_async_copy(p[0], held.at[n], arrive.at[n]) for n, p in enumerate(pairs)]
+    outward = [pltpu.make_async_copy(held.at[n], p[1], leave.at[n]) for n, p in enumerate(pairs)]
+    for c in inward:
+        c.start()
+    for n in range(4):
+        inward[n].wait()
+        outward[n].start()
+    for c in outward:
+        c.wait()
 
 
 def on_device(query_rows, key_rows, value_rows, scale_index, norm_gain, cotangent):
@@ -534,8 +623,9 @@
         pltpu.VMEM((SLOTS, COLS), BF16),
         pltpu.VMEM((COARSE, COLS), F32),
         pltpu.VMEM((COARSE, COLS), F32),
-        pltpu.VMEM((RIM, HEAD_DIM), F32),
-        pltpu.VMEM((RIM, HEAD_DIM), F32),
+        pltpu.VMEM((HEADS, 1, FINE), F32),
+        pltpu.VMEM((HEADS, 1, FINE), F32),
+        pltpu.VMEM((HEADS, HEAD_DIM, FINE), F32),
         pltpu.VMEM((HEADS, FINE, HEAD_DIM), F32),
         pltpu.VMEM((HEADS, FINE, HEAD_DIM), F32),
         pltpu.VMEM((2, BLOCK, COLS), BF16),
@@ -553,7 +643,7 @@
         pltpu.SemaphoreType.DMA((COPIES,)),
         pltpu.SemaphoreType.DMA((COPIES,)),
     ]
-    return tuple(pl.pallas_call(
+    results = pl.pallas_call(
         kernel,
         out_shape=[full] * 4,
         in_specs=[whole] * 6,
@@ -562,7 +652,19 @@
         compiler_params=pltpu.CompilerParams(
             collective_id=0, has_side_effects=True, vmem_limit_bytes=56 * 1024 * 1024
         ),
-    )(query_rows, key_rows, value_rows, cotangent, norm_gain, scale_index))
+    )(query_rows, key_rows, value_rows, cotangent, norm_gain, scale_index)
+    anywhere = pl.BlockSpec(memory_space=pl.ANY)
+    return tuple(pl.pallas_call(
+        deliver,
+        out_shape=[full] * 4,
+        in_specs=[anywhere] * 4,
+        out_specs=[anywhere] * 4,
+        scratch_shapes=[
+            pltpu.VMEM((4, FINE + CO, COLS), BF16),
+            pltpu.SemaphoreType.DMA((4,)),
+            pltpu.SemaphoreType.DMA((4,)),
+        ],
+    )(*results))
 
 
 def solution(mesh):

time: 116 us -> 109 us (0.940)
  the two profiles are of different devices: /device:TPU:1 before, /device:TPU:114 now
where the time goes in v3:
time: 109 us
  Pallas kernels  108 us (99%)
    pallas_call x1, Pallas kernels, on_device(): pl.pallas_call(kernel, out_shape=[full] * 4, in_specs=[whole] * 6, out_sp...  105 us
    pallas_call x1, Pallas kernels, on_device(): pl.pallas_call(deliver, out_shape=[full] * 4, in_specs=[anywhere] * 4, ou...  2.72 us

profile of v3, /device:TPU:114, one launch (start us, length us, event | category | flops | bytes accessed | tf_op | source)
XLA Modules:
  0.0 108.7 jit_solution(9112176235509086370)
XLA Ops:
  0.6 105.2 %shard_map.93 = (bf16[392,896]{1,0:T(8,128)(2,1)}, bf16[392,896]{1,0:T(8,128)(2,1)}, bf16[392,896]{1,0:T(8,128)(2,1)}, bf16[392,896]{1,0:T(8,128)(2,1)}) custom-call(bf16[392,896]{1,0:T(8,128)(2,1)} %q.1, bf16[392,896]{1,0:T(8,128)(2,1)} %k.1, bf16[392,896]{1,0:T(8,128)(2,1)} %v.1, bf16[392,896]{1,0:T(8,128)(2,1)} %cot.1, f32[896]{0:T(1024)} %gain_ref.1, ...), custom_call_target="tpu_custom_call" | custom-call | tf_op jit(solution)/shard_map/pallas_call | solution.py:646
  105.8 2.7 %shard_map.94 = (bf16[392,896]{1,0:T(8,128)(2,1)}, bf16[392,896]{1,0:T(8,128)(2,1)}, bf16[392,896]{1,0:T(8,128)(2,1)}, bf16[392,896]{1,0:T(8,128)(2,1)}) custom-call(bf16[392,896]{1,0:T(8,128)(2,1)} %get-tuple-element.8.a, bf16[392,896]{1,0:T(8,128)(2,1)} %get-tuple-element.9.b, bf16[392,896]{1,0:T(8,128)(2,1)} %get-tuple-element.10.c, ...), custom_call_target="tpu_custom_call" | custom-call | tf_op jit(solution)/shard_map/pallas_call | solution.py:657

commit v4 on v3

--- a/solution.py
+++ b/solution.py
@@ -30,8 +30,10 @@
 
 CHUNKS = 4
 CHUNK = WIN // CHUNKS
+HALF = WIN // 2
+EARLY = (0, 1)
 HALO_K = 0
-HALO_V = HALO_K + 2
+HALO_V = HALO_K + 4
 HOP = HALO_V + 2 * CHUNKS
 AG_Z = HOP + 2 * CHUNKS
 AG_Y = AG_Z + 3
@@ -136,14 +138,19 @@
         c.start()
         pending.append(c)
 
-    def depart(side, number, hop, src, via, dst):
+    def depart_edge(side, number, hop, src, via, dst):
         @pl.when(edges[side])
         def _():
             copy(src, via, hop, first_hop[side]).start()
 
+    def depart_inner(side, number, hop, src, via, dst):
         @pl.when(jnp.logical_not(edges[side]))
         def _():
             copy(src, dst, number, beside[side]).start()
+
+    def depart(*transfer):
+        depart_edge(*transfer)
+        depart_inner(*transfer)
 
     def pass_on(side, number, hop, via, dst):
         @pl.when(relaying[side])
@@ -184,13 +191,22 @@
             v.at[a : a + CHUNK], relay.at[c], vrim.at[b : b + CHUNK],
         )
 
-    for c in range(CHUNKS):
+    for c in EARLY:
         for side in range(2):
-            depart(side, *chunk(side, c))
+            depart_edge(side, *chunk(side, c))
     halves = (
-        (k, krim, slice(WIN, 2 * WIN), slice(0, WIN), right),
-        (k, krim, slice(0, WIN), slice(WIN + FINE, RIM), left),
+        (k, krim, slice(WIN, WIN + HALF), slice(0, HALF), right),
+        (k, krim, slice(0, HALF), slice(WIN + FINE, WIN + FINE + HALF), left),
+        (k, krim, slice(WIN + HALF, 2 * WIN), slice(HALF, WIN), right),
+        (k, krim, slice(HALF, WIN), slice(WIN + FINE + HALF, RIM), left),
     )
+
+    def send_keys(n, when):
+        src, dst, a, b, peer = halves[n]
+
+        @pl.when(when)
+        def _():
+            copy(src.at[a], dst.at[b], HALO_K + n, peer).start()
 
     def pass_chunk(c):
         for side in range(2):
@@ -238,9 +254,8 @@
         start(block, block, AG_Y + d - 1, ys[d - 1])
     start(block, block, AG_X + 0, xr)
     start(block, block, AG_X + 4, xl)
-    for n, (src, dst, a, b, peer) in enumerate(halves):
-        start(src.at[a], dst.at[b], HALO_K + n, peer)
     pass_chunk(0)
+    pass_chunk(1)
     every_head(own_keys, 0, 2, 4)
 
     level = jnp.broadcast_to(levels[...].astype(F32).reshape(1, COARSE), (CO, COARSE))
@@ -252,7 +267,6 @@
     order = (lane // 128) * 128 + ((lane // 8) % 4) * 32 + ((lane // 32) % 4) * 8 + lane % 8
     allowed = order.astype(F32) < jnp.concatenate([seen] * (SLOTS // CO), axis=0)
     lmask[...] = jnp.where(allowed, 0.0, NEG)
-    pass_chunk(1)
 
     def prepare(h, _):
         cols = head_cols(h)
@@ -266,7 +280,14 @@
         copy(block, block, AG_Y + d - 1, ys[d - 1]).wait_recv()
         start(block, block, AG_X + d, xr)
         start(block, block, AG_X + 4 + d, xl)
-    pass_chunk(2)
+    for c in range(CHUNKS):
+        for side in range(2):
+            if c in EARLY:
+                depart_inner(side, *chunk(side, c))
+            else:
+                depart(side, *chunk(side, c))
+    for n in range(4):
+        send_keys(n, y >= 0)
     every_head(own_keys, 0, 4, HEADS)
     every_head(prepare, 0, 0, HEADS)
     qd[...] = spread(tail(q)).astype(BF16)
@@ -280,8 +301,8 @@
         copy(from_right, from_right, AG_X + 4 + d, xl).wait_recv()
         if d in (1, 3):
             start(from_right, from_right, AG_F + d, xl)
-        if d == 1:
-            pass_chunk(3)
+        if d in (0, 1):
+            pass_chunk(2 + d)
     for d in (0, 1, 3, 2):
         far = line((x + 2) % 4, (y + 4 - d) % 4)
         copy(far, far, AG_F + d, xr if d in (0, 2) else xl).wait_recv()
@@ -319,7 +340,7 @@
     crossed_c = jnp.sum(attended_c * gained_c, axis=1, keepdims=True)
 
     for n, (src, dst, a, b, peer) in enumerate(halves):
-        copy(src.at[a], dst.at[b], HALO_K + n, peer).wait_recv()
+        copy(src.at[a], dst.at[b], HALO_K + n, peer).wait()
     for c in range(CHUNKS):
         for side in range(2):
             number, _, _, _, dst = chunk(side, c)
@@ -411,9 +432,7 @@
         q1, k1, v1 = gradients(h, 1, 128, 192)
         q2, k2, v2 = gradients(h, 1, 576, 640)
         q3, k3, v3 = gradients(h, 2, 576, 768)
-        dqt[h, :, 0:BLOCK] = q0
-        dqt[h, :, BLOCK : 2 * BLOCK] = q1 + q2
-        dqt[h, :, 2 * BLOCK : FINE] = q3
+        dqt[h] = jnp.concatenate([q0, q1 + q2, q3], axis=1)
         for n, (a, b, c, d) in enumerate(((k0, k1, k2, k3), (v0, v1, v2, v3))):
             back_out[1, h, n, 0:128] = a[0:128].astype(BF16)
             back_out[1, h, n, 128:192] = (a[128:192] + b).astype(BF16)
@@ -472,24 +491,23 @@
     opp_out[1] = gv[rows].astype(BF16)
     start(opp_out.at[0], opp_in.at[0], RS_OPP, xr)
     start(opp_out.at[1], opp_in.at[1], RS_OPP + 1, xl)
-    pass_back(0, 2)
+    pass_back(0, 3)
     rows_r = coarse_block((x + 1) % 4)
-    pass_back(2, 4)
-    rows_l = coarse_block((x + 3) % 4)
     copy(opp_out.at[0], opp_in.at[0], RS_OPP, xr).wait_recv()
     x_out[0] = (gk[rows_r] + opp_in[0].astype(F32)).astype(BF16)
     x_out[1] = gv[rows_r].astype(BF16)
     start(x_out.at[0], x_in.at[0], RS_X, xr)
     start(x_out.at[1], x_in.at[1], RS_X + 1, xr)
+    pass_back(3, 4)
+    rows_l = coarse_block((x + 3) % 4)
     copy(opp_out.at[1], opp_in.at[1], RS_OPP + 1, xl).wait_recv()
     x_out[2] = gk[rows_l].astype(BF16)
     x_out[3] = (gv[rows_l] + opp_in[1].astype(F32)).astype(BF16)
     start(x_out.at[2], x_in.at[2], RS_X + 2, xl)
     start(x_out.at[3], x_in.at[3], RS_X + 3, xl)
-    pass_back(4, 6)
-
+    pass_back(4, 5)
     own = coarse_block(x)
-    pass_back(6, 7)
+    pass_back(5, 6)
 
     def own_grads(h, _):
         for b in range(3):
@@ -509,6 +527,7 @@
         return 0
 
     every_head(own_grads, 0, 0, HEADS)
+    pass_back(6, 7)
 
     for n in range(4):
         copy(x_out.at[n], x_in.at[n], RS_X + n, xr if n < 2 else xl).wait_recv()
@@ -536,8 +555,8 @@
         of_q[:, cols] = jnp.concatenate(queries + [coarse_row[1, :, cols]], axis=0).astype(BF16)
         return 0
 
+
     every_head(finish, 0, 0, HEADS)
-
     for d in (1, 2, 3):
         copy(y_out.at[d - 1], y_in.at[d - 1], RS_Y + d - 1, ys[d - 1]).wait_recv()
     here = piece(y, 0, 32)
@@ -548,14 +567,14 @@
         )
     for d in (1, 2, 3):
         there = piece(y, (z + d) % 4, CO)
-        z_out[d - 1, 0] = gk[there]
-        z_out[d - 1, 1] = gv[there]
+        z_out[d - 1] = jnp.concatenate([gk[there], gv[there]], axis=0).astype(BF16)
         start(z_out.at[d - 1], z_in.at[d - 1], RS_Z + d - 1, zs[d - 1])
     for d in (1, 2, 3):
         copy(z_out.at[d - 1], z_in.at[d - 1], RS_Z + d - 1, zs[d - 1]).wait_recv()
     here = piece(y, z, CO)
-    coarse_row[0] = gk[here] + z_in[0, 0] + z_in[1, 0] + z_in[2, 0]
-    coarse_row[1] = gv[here] + z_in[0, 1] + z_in[1, 1] + z_in[2, 1]
+    arrived = z_in[0].astype(F32) + z_in[1].astype(F32) + z_in[2].astype(F32)
+    coarse_row[0] = gk[here] + arrived[0:CO]
+    coarse_row[1] = gv[here] + arrived[CO:]
 
     def fold(h, _):
         cols = head_cols(h)
@@ -634,8 +653,8 @@
         pltpu.VMEM((4, BLOCK, COLS), BF16),
         pltpu.VMEM((3, 2, 32, COLS), BF16),
         pltpu.VMEM((3, 2, 32, COLS), BF16),
-        pltpu.VMEM((3, 2, CO, COLS), F32),
-        pltpu.VMEM((3, 2, CO, COLS), F32),
+        pltpu.VMEM((3, 2 * CO, COLS), BF16),
+        pltpu.VMEM((3, 2 * CO, COLS), BF16),
         pltpu.VMEM((2, HEADS, 2, WIN, HEAD_DIM), BF16),
         pltpu.VMEM((2, HEADS, 2, WIN, HEAD_DIM), BF16),
         pltpu.VMEM((CHUNKS, CHUNK, COLS), BF16),

time: 109 us -> 103 us (0.945)
  the two profiles are of different devices: /device:TPU:114 before, /device:TPU:80 now
where the time goes in v4:
time: 103 us
  Pallas kernels  102 us (99%)
    pallas_call x1, Pallas kernels, on_device(): pl.pallas_call(kernel, out_shape=[full] * 4, in_specs=[whole] * 6, out_sp...  99.4 us
    pallas_call x1, Pallas kernels, on_device(): pl.pallas_call(deliver, out_shape=[full] * 4, in_specs=[anywhere] * 4, ou...  2.72 us

profile of v4, /device:TPU:80, one launch (start us, length us, event | category | flops | bytes accessed | tf_op | source)
XLA Modules:
  0.0 102.9 jit_solution(11674442619395604617)
XLA Ops:
  0.6 99.4 %shard_map.93 = (bf16[392,896]{1,0:T(8,128)(2,1)}, bf16[392,896]{1,0:T(8,128)(2,1)}, bf16[392,896]{1,0:T(8,128)(2,1)}, bf16[392,896]{1,0:T(8,128)(2,1)}) custom-call(bf16[392,896]{1,0:T(8,128)(2,1)} %q.1, bf16[392,896]{1,0:T(8,128)(2,1)} %k.1, bf16[392,896]{1,0:T(8,128)(2,1)} %v.1, bf16[392,896]{1,0:T(8,128)(2,1)} %cot.1, f32[896]{0:T(1024)} %gain_ref.1, ...), custom_call_target="tpu_custom_call" | custom-call | tf_op jit(solution)/shard_map/pallas_call | solution.py:665
  100.0 2.7 %shard_map.94 = (bf16[392,896]{1,0:T(8,128)(2,1)}, bf16[392,896]{1,0:T(8,128)(2,1)}, bf16[392,896]{1,0:T(8,128)(2,1)}, bf16[392,896]{1,0:T(8,128)(2,1)}) custom-call(bf16[392,896]{1,0:T(8,128)(2,1)} %get-tuple-element.8.a, bf16[392,896]{1,0:T(8,128)(2,1)} %get-tuple-element.9.b, bf16[392,896]{1,0:T(8,128)(2,1)} %get-tuple-element.10.c, ...), custom_call_target="tpu_custom_call" | custom-call | tf_op jit(solution)/shard_map/pallas_call | solution.py:676

commit v5 on v4

--- a/solution.py
+++ b/solution.py
@@ -432,7 +432,7 @@
         q1, k1, v1 = gradients(h, 1, 128, 192)
         q2, k2, v2 = gradients(h, 1, 576, 640)
         q3, k3, v3 = gradients(h, 2, 576, 768)
-        dqt[h] = jnp.concatenate([q0, q1 + q2, q3], axis=1)
+        dqt[h] = dqt[h] + jnp.concatenate([q0, q1 + q2, q3], axis=1)
         for n, (a, b, c, d) in enumerate(((k0, k1, k2, k3), (v0, v1, v2, v3))):
             back_out[1, h, n, 0:128] = a[0:128].astype(BF16)
             back_out[1, h, n, 128:192] = (a[128:192] + b).astype(BF16)
@@ -455,7 +455,6 @@
 
         every_head(body, 0, first, last)
 
-    every_head(halo_grads, 0, 0, HEADS)
 
     scores = nt(qd[...], kc[...]) * (SCALING * LOG2E) + lmask[...]
     probs = jnp.exp2(scores - log_c)
@@ -486,29 +485,28 @@
         every_head(body, 0, 0, HEADS)
         return rows
 
+    dqt[...] = jnp.zeros_like(dqt)
     rows = coarse_block((x + 2) % 4)
     opp_out[0] = gk[rows].astype(BF16)
     opp_out[1] = gv[rows].astype(BF16)
     start(opp_out.at[0], opp_in.at[0], RS_OPP, xr)
     start(opp_out.at[1], opp_in.at[1], RS_OPP + 1, xl)
-    pass_back(0, 3)
     rows_r = coarse_block((x + 1) % 4)
     copy(opp_out.at[0], opp_in.at[0], RS_OPP, xr).wait_recv()
     x_out[0] = (gk[rows_r] + opp_in[0].astype(F32)).astype(BF16)
     x_out[1] = gv[rows_r].astype(BF16)
     start(x_out.at[0], x_in.at[0], RS_X, xr)
     start(x_out.at[1], x_in.at[1], RS_X + 1, xr)
-    pass_back(3, 4)
     rows_l = coarse_block((x + 3) % 4)
     copy(opp_out.at[1], opp_in.at[1], RS_OPP + 1, xl).wait_recv()
     x_out[2] = gk[rows_l].astype(BF16)
     x_out[3] = (gv[rows_l] + opp_in[1].astype(F32)).astype(BF16)
     start(x_out.at[2], x_in.at[2], RS_X + 2, xl)
     start(x_out.at[3], x_in.at[3], RS_X + 3, xl)
-    pass_back(4, 5)
+    every_head(halo_grads, 0, 0, HEADS)
     own = coarse_block(x)
-    pass_back(5, 6)
-
+
+    pass_back(0, 2)
     def own_grads(h, _):
         for b in range(3):
             first, last = OWN[b]
@@ -527,8 +525,8 @@
         return 0
 
     every_head(own_grads, 0, 0, HEADS)
-    pass_back(6, 7)
-
+
+    pass_back(2, 4)
     for n in range(4):
         copy(x_out.at[n], x_in.at[n], RS_X + n, xr if n < 2 else xl).wait_recv()
     gk[own] = gk[own] + x_in[0].astype(F32) + x_in[2].astype(F32)
@@ -556,6 +554,7 @@
         return 0
 
 
+    pass_back(4, 5)
     every_head(finish, 0, 0, HEADS)
     for d in (1, 2, 3):
         copy(y_out.at[d - 1], y_in.at[d - 1], RS_Y + d - 1, ys[d - 1]).wait_recv()
@@ -569,6 +568,7 @@
         there = piece(y, (z + d) % 4, CO)
         z_out[d - 1] = jnp.concatenate([gk[there], gv[there]], axis=0).astype(BF16)
         start(z_out.at[d - 1], z_in.at[d - 1], RS_Z + d - 1, zs[d - 1])
+    pass_back(5, 7)
     for d in (1, 2, 3):
         copy(z_out.at[d - 1], z_in.at[d - 1], RS_Z + d - 1, zs[d - 1]).wait_recv()
     here = piece(y, z, CO)

time: 103 us -> 101 us (0.981)
  the two profiles are of different devices: /device:TPU:80 before, /device:TPU:1 now
where the time goes in v5:
time: 101 us; the launch traced here: 99.6 us
  Pallas kernels  98.8 us (98%)
    pallas_call x1, Pallas kernels, on_device(): pl.pallas_call(kernel, out_shape=[full] * 4, in_specs=[whole] * 6, out_sp...  96.1 us
    pallas_call x1, Pallas kernels, on_device(): pl.pallas_call(deliver, out_shape=[full] * 4, in_specs=[anywhere] * 4, ou...  2.72 us

profile of v5, /device:TPU:1, one launch (start us, length us, event | category | flops | bytes accessed | tf_op | source)
XLA Modules:
  0.0 99.6 jit_solution(2550396397313020220)
XLA Ops:
  0.6 96.1 %shard_map.93 = (bf16[392,896]{1,0:T(8,128)(2,1)}, bf16[392,896]{1,0:T(8,128)(2,1)}, bf16[392,896]{1,0:T(8,128)(2,1)}, bf16[392,896]{1,0:T(8,128)(2,1)}) custom-call(bf16[392,896]{1,0:T(8,128)(2,1)} %q.1, bf16[392,896]{1,0:T(8,128)(2,1)} %k.1, bf16[392,896]{1,0:T(8,128)(2,1)} %v.1, bf16[392,896]{1,0:T(8,128)(2,1)} %cot.1, f32[896]{0:T(1024)} %gain_ref.1, ...), custom_call_target="tpu_custom_call" | custom-call | tf_op jit(solution)/shard_map/pallas_call | solution.py:665
  96.7 2.7 %shard_map.94 = (bf16[392,896]{1,0:T(8,128)(2,1)}, bf16[392,896]{1,0:T(8,128)(2,1)}, bf16[392,896]{1,0:T(8,128)(2,1)}, bf16[392,896]{1,0:T(8,128)(2,1)}) custom-call(bf16[392,896]{1,0:T(8,128)(2,1)} %get-tuple-element.8.a, bf16[392,896]{1,0:T(8,128)(2,1)} %get-tuple-element.9.b, bf16[392,896]{1,0:T(8,128)(2,1)} %get-tuple-element.10.c, ...), custom_call_target="tpu_custom_call" | custom-call | tf_op jit(solution)/shard_map/pallas_call | solution.py:676

commit v6 on v5

--- a/solution.py
+++ b/solution.py
@@ -334,6 +334,7 @@
     total = jnp.sum(weights, axis=1, keepdims=True)
     wide = nn(weights.astype(BF16), vc[...]) / total
     log_c = peak + jnp.log2(total)
+    probs = jnp.exp2(scores - log_c)
     attended_c = collect(wide).astype(BF16).astype(F32)
     gained_c = tail(cot) * gain
     squares_c = jnp.sum(attended_c * attended_c, axis=1, keepdims=True)
@@ -456,8 +457,6 @@
         every_head(body, 0, first, last)
 
 
-    scores = nt(qd[...], kc[...]) * (SCALING * LOG2E) + lmask[...]
-    probs = jnp.exp2(scores - log_c)
     grad_probs = nt(dod[...], vc[...])
     grad_scores = (probs * (grad_probs - delta_c)).astype(BF16)
     query_c = collect(nn(grad_scores, kc[...])) * SCALING

time: 101 us -> 101 us (level)
  no operation moved by 1% of the time
where the time goes in v6:
time: 101 us; the launch traced here: 99.6 us
  Pallas kernels  98.8 us (98%)
    pallas_call x1, Pallas kernels, on_device(): pl.pallas_call(kernel, out_shape=[full] * 4, in_specs=[whole] * 6, out_sp...  96.1 us
    pallas_call x1, Pallas kernels, on_device(): pl.pallas_call(deliver, out_shape=[full] * 4, in_specs=[anywhere] * 4, ou...  2.72 us

profile of v6, /device:TPU:1, one launch (start us, length us, event | category | flops | bytes accessed | tf_op | source)
XLA Modules:
  0.0 99.6 jit_solution(17621346608552141027)
XLA Ops:
  0.6 96.1 %shard_map.93 = (bf16[392,896]{1,0:T(8,128)(2,1)}, bf16[392,896]{1,0:T(8,128)(2,1)}, bf16[392,896]{1,0:T(8,128)(2,1)}, bf16[392,896]{1,0:T(8,128)(2,1)}) custom-call(bf16[392,896]{1,0:T(8,128)(2,1)} %q.1, bf16[392,896]{1,0:T(8,128)(2,1)} %k.1, bf16[392,896]{1,0:T(8,128)(2,1)} %v.1, bf16[392,896]{1,0:T(8,128)(2,1)} %cot.1, f32[896]{0:T(1024)} %gain_ref.1, ...), custom_call_target="tpu_custom_call" | custom-call | tf_op jit(solution)/shard_map/pallas_call | solution.py:664
  96.7 2.7 %shard_map.94 = (bf16[392,896]{1,0:T(8,128)(2,1)}, bf16[392,896]{1,0:T(8,128)(2,1)}, bf16[392,896]{1,0:T(8,128)(2,1)}, bf16[392,896]{1,0:T(8,128)(2,1)}) custom-call(bf16[392,896]{1,0:T(8,128)(2,1)} %get-tuple-element.8.a, bf16[392,896]{1,0:T(8,128)(2,1)} %get-tuple-element.9.b, bf16[392,896]{1,0:T(8,128)(2,1)} %get-tuple-element.10.c, ...), custom_call_target="tpu_custom_call" | custom-call | tf_op jit(solution)/shard_map/pallas_call | solution.py:675
